TPU v7x, 32 devices: a whole 2x2x4 slice. The times are simulated.
32 devices in a mesh: group: 4 (over y, core), space: 8 (over z, x).
Axes of the slice: x: 2, y: 2, z: 4, core: 2. Of those that a mesh axis runs over, the one named last changes fastest.
Arguments:
- initial_state: float32 [32, 3, 32, 1024], P(('group', 'space')), may hold values from -3 to 3
- phases: int32 [32, 32, 1024], P(('group', 'space')), may hold values from 0 to 2
- brick_coords: int32 [32, 3], P(('group', 'space')), may hold values from -1 to 7, as said below
- neighbours: int32 [32, 6], P(('group', 'space')), may hold values from -1 to 31, as said below
- source: float32 [32, 3, 32, 1024], P(('group', 'space'))
- coarse_inverse: float32 [4, 24, 24], P('group', 'space')
Outputs:
- final_state: float32 [32, 3, 32, 1024], P(('group', 'space'))
Inputs may be any that keep to these rules, and one draw needn't show every extreme that they name: `brick_coords`: an occupied slot of device (g, s) holds the brick at x place bx, y = s, z = g; each x place occurs at most once on a device; an empty slot is -1 in all three; device (0, 0), every device with s = 7, and device (3, 6) have every slot occupied. Global slot = device index (group index * 8 + space index) + slot. The -x and +x neighbours lie on the same device, -y and +y on the device one step lower or higher along space, -z and +z one step lower or higher along group, always at the same x place; a face has a neighbour exactly where that brick is occupied; the relation is symmetric; empty slots have -1 everywhere.
All inputs are finite; a program needn't handle non-finite values.
Results may differ from a plain program's by a relative error of at most 0.0003.
Values sent between devices are 32-bit elements; how exact they have to be, the bound alone decides.
A program may use at most 64 MiB of HBM per device.

v0:
```python
import functools

import jax
import jax.numpy as jnp
from jax import lax
from jax.experimental import pallas as pl
from jax.experimental.pallas import tpu as pltpu
from jax.sharding import PartitionSpec as P

NEWTON = 2
SMOOTH = 4
ROUNDS = SMOOTH + 1
E = 32
TILES = 8
PAD = 8
OMEGA = 0.8
MESH = pl.DeviceIdType.MESH
F32 = jnp.float32


def roll(x, shift):
    shift = shift % 128
    return x if shift == 0 else pltpu.roll(x, shift, 1)


def place(f, t):
    return (0, 16 * f + 2 * t) if f < 2 else (1, 2 * t)


def kernel(
    n, m,
    coords_in, links_in, inverse_in, state_hbm, phase_hbm, source_hbm, out,
    coords, links, inverse, state_in, phase_in, source_in, fetch,
    state, upd, base, gain, mix, diag, source, phase,
    send, recv, squares_a, squares_b, coarse, weights,
    face_send, face_recv, a_send, a_recv, b_send, b_recv, c_send, c_recv,
):
    me_s = lax.axis_index("space")
    me_g = lax.axis_index("group")
    lane = lax.broadcasted_iota(jnp.int32, (E, 128), 1)
    block = lane // 32
    depth = lane % 32
    first = depth == 0
    last = depth == 31
    edge = first | last
    even = lane % 2 == 0

    fetches = [
        pltpu.make_async_copy(a, b, fetch.at[i])
        for i, (a, b) in enumerate((
            (state_hbm, state_in), (coords_in, coords), (links_in, links),
            (phase_hbm, phase_in), (source_hbm, source_in), (inverse_in, inverse),
        ))
    ]
    for copy in fetches:
        copy.start()

    targets = (("space", me_s, 1, n), ("space", me_s, -1, n), ("group", me_g, 1, m), ("group", me_g, -1, m))

    def has(axis, me, step, size):
        return me + step < size if step > 0 else me + step >= 0

    barrier = pltpu.get_barrier_semaphore()
    for axis, me, size in (("space", me_s, n), ("group", me_g, m)):
        for d in range(1, size):
            pl.semaphore_signal(barrier, inc=1, device_id={axis: lax.rem(me + d, size)}, device_id_type=MESH)

    def face_copy(r, d):
        axis, me, step, size = targets[d]
        return pltpu.make_async_remote_copy(
            src_ref=send.at[r, d], dst_ref=recv.at[r, d],
            send_sem=face_send.at[r, d], recv_sem=face_recv.at[r, d],
            device_id={axis: jnp.clip(me + step, 0, size - 1)}, device_id_type=MESH)

    def source_of(d):
        axis, me, step, size = targets[d]
        return has(axis, me, -step, size)

    def start_faces(r, which):
        for d in which:
            @pl.when(has(*targets[d]))
            def _():
                face_copy(r, d).start()

    def wait_faces(r, which):
        for d in which:
            @pl.when(source_of(d))
            def _():
                face_copy(r, d).wait_recv()

    def gather_copy(buf, ss, rs, k, d, axis, me, size):
        return pltpu.make_async_remote_copy(
            src_ref=buf.at[k, 0], dst_ref=buf.at[k, d],
            send_sem=ss.at[k, d], recv_sem=rs.at[k, d],
            device_id={axis: lax.rem(me + d, size)}, device_id_type=MESH)

    over_a = (squares_a, a_send, a_recv)
    over_b = (squares_b, b_send, b_recv)
    over_c = (coarse, c_send, c_recv)

    def gather_start(bufs, k, axis, me, size):
        for d in range(1, size):
            gather_copy(*bufs, k, d, axis, me, size).start()

    def gather_wait(bufs, k, axis, me, size):
        for d in range(1, size):
            gather_copy(*bufs, k, d, axis, me, size).wait_recv()


    def swap4(a):
        low = block < 2
        t0 = jnp.where(low, a[0], roll(a[2], 64))
        t2 = jnp.where(low, roll(a[0], 64), a[2])
        t1 = jnp.where(low, a[1], roll(a[3], 64))
        t3 = jnp.where(low, roll(a[1], 64), a[3])
        ev = block % 2 == 0
        return (jnp.where(ev, t0, roll(t1, 32)), jnp.where(ev, roll(t0, 96), t1),
                jnp.where(ev, t2, roll(t3, 32)), jnp.where(ev, roll(t2, 96), t3))

    def spread_in(load):
        tiles = [None] * 8
        for h in range(2):
            got = swap4([load(2 * k + h) for k in range(4)])
            for r in range(4):
                tiles[4 * h + r] = got[r]
        return tiles

    fetches[1].wait()
    fetches[2].wait()
    occupied = coords[0, 0] >= 0
    mask = jnp.where(occupied, 1.0, 0.0).astype(F32)
    wall = coords[0, 0].astype(F32) + coords[0, 1].astype(F32) / n + coords[0, 2].astype(F32) / m - 1.0
    linked = [links[0, 2 + d] >= 0 for d in range(4)]

    zero_rows = jnp.zeros((PAD, 128), F32)
    for f in range(3):
        for t in range(TILES):
            edge_rows = zero_rows if f < 2 else zero_rows + wall
            state[f, t, 0:PAD] = edge_rows
            state[f, t, PAD + E:] = edge_rows
            for b in range(2):
                upd[b, f, t, 0:PAD] = zero_rows
                upd[b, f, t, PAD + E:] = zero_rows
    fetches[0].wait()
    for f in range(3):
        tiles = spread_in(lambda t: state_in[f, :, t * 128:(t + 1) * 128])
        for t in range(TILES):
            state[f, t, PAD:PAD + E] = tiles[t] * mask

    def pack_z(planes, f, t, c):
        q, j = place(f, t)
        part = roll(jnp.where(edge, c, 0.0), j)
        planes[q] = part if planes[q] is None else planes[q] + part

    def y_planes(ends):
        up = jnp.where(block == 0, roll(ends[0][1], -96), jnp.where(block == 1, roll(ends[1][1], -64), roll(ends[2][1], -32)))
        down = jnp.where(block == 0, ends[0][0], jnp.where(block == 1, roll(ends[1][0], 32), roll(ends[2][0], 64)))
        return [up, down]

    def z_planes(planes):
        q0, q1 = planes
        return [jnp.where(even, roll(q1, -1), q0), jnp.where(even, q0, roll(q1, 1))]

    def post_y(r, ends):
        send[r, 0], send[r, 1] = y_planes(ends)
        start_faces(r, (0, 1))

    def post_z(r, planes):
        send[r, 2], send[r, 3] = z_planes(planes)
        start_faces(r, (2, 3))

    def walled(r, d, walls):
        got = recv[r, d]
        if not walls:
            return got, got
        return jnp.where(linked[d], got, 0.0), jnp.where(linked[d], got, wall)

    def ghosts_z(r, walls):
        wait_faces(r, (2, 3))
        low, solid_low = walled(r, 2, walls)
        high, solid_high = walled(r, 3, walls)
        c0 = jnp.where(even, high, roll(low, 66))
        c1 = jnp.where(even, roll(solid_high, -1), roll(solid_low, 67))
        return c0, c1

    def ghosts_y(r, walls):
        wait_faces(r, (0, 1))
        low = walled(r, 0, walls)
        high = walled(r, 1, walls)
        lows = [roll(low[f // 2], -32 * f) for f in range(3)]
        highs = [roll(high[f // 2], 96 - 32 * f) for f in range(3)]
        return lows, highs

    inside = tuple(range(1, TILES - 1))
    outside = (0, TILES - 1)

    def around(ref, f, t, ghosts):
        planes, (lows, highs) = ghosts
        c = ref[f, t, PAD:PAD + E]
        total = ref[f, t, PAD - 1:PAD - 1 + E] + ref[f, t, PAD + 1:PAD + 1 + E]
        if t > 0:
            total = total + ref[f, t - 1, PAD:PAD + E]
        else:
            total = total + jnp.where(block == 0, lows[f], roll(ref[f, TILES - 1, PAD:PAD + E], 32))
        if t < TILES - 1:
            total = total + ref[f, t + 1, PAD:PAD + E]
        else:
            total = total + jnp.where(block == 3, highs[f], roll(ref[f, 0, PAD:PAD + E], -32))
        q, j = place(f, t)
        ghost = roll(planes[q], 31 - j)
        total = total + jnp.where(last, ghost, roll(c, -1)) + jnp.where(first, ghost, roll(c, 1))
        return c, total

    def pack_state():
        planes, ends = [None, None], []
        for f in range(3):
            tiles = [state[f, t, PAD:PAD + E] for t in range(TILES)]
            for t in range(TILES):
                pack_z(planes, f, t, tiles[t])
            ends.append((tiles[0], tiles[TILES - 1]))
        return planes, ends

    planes, ends = pack_state()
    pl.semaphore_wait(barrier, n + m - 2)
    post_y(0, ends)
    post_z(0, planes)

    rows8 = lax.broadcasted_iota(jnp.int32, (8, 128), 0)
    blank = jnp.zeros((E, 128), F32)
    for d in range(4):
        @pl.when(jnp.logical_not(source_of(d)))
        def _():
            for r in range(NEWTON * ROUNDS):
                recv[r, d] = blank
    for copy in fetches[3:]:
        copy.wait()
    for f in range(3):
        tiles = spread_in(lambda t: source_in[f, :, t * 128:(t + 1) * 128])
        for t in range(TILES):
            source[f, t] = tiles[t]
    tiles = spread_in(lambda t: phase_in[:, t * 128:(t + 1) * 128])
    for t in range(TILES):
        phase[t] = tiles[t]
    for d in range(n):
        owner = lax.rem(me_s - d + n, n)
        for i in range(3):
            v = [inverse[i, 0, 3 * owner + f] for f in range(3)]
            weights[i, d] = jnp.where(rows8 == 0, v[0], jnp.where(rows8 == 1, v[1], jnp.where(rows8 == 2, v[2], 0.0)))

    def fold(x):
        return x[0:8] + x[8:16] + x[16:24] + x[24:32]

    def sweep(k, carry):
        r0 = k * ROUNDS
        planes_in = ghosts_z(r0, True)
        ghosts = (planes_in, (None, None))
        planes, ends = [None, None], [[None, None] for _ in range(3)]
        square = jnp.zeros((E, 128), F32)
        for t in inside + outside:
            if t == 0:
                ghosts = (planes_in, ghosts_y(r0, True))
            label = phase[t]
            pore = label == 0
            active = label == 1
            conduct = (jnp.where(pore, 1.0, 0.2), jnp.where(pore, 1.0, 0.1),
                       jnp.where(pore, 0.05, jnp.where(active, 0.5, 1.5)))
            rates = jnp.where(pore, 0.0, jnp.where(active, 0.3, 0.02))
            pairs = [around(state, f, t, ghosts) for f in range(3)]
            c, e, s = (p[0] for p in pairs)
            eta = s - e - 0.5 * c
            forward = jnp.exp(0.5 * eta)
            backward = jnp.exp(-0.5 * eta)
            current = rates * (forward - backward)
            slope = 0.5 * rates * (forward + backward)
            react = (-0.5 * current, -current, current)
            for f in range(3):
                v, total = pairs[f]
                misfit = mask * (0.5 * v + conduct[f] * (6.0 * v - total) + react[f] - source[f, t])
                square = square + misfit * misfit
                dg = 0.5 + 6.0 * conduct[f] + (0.25 * slope if f == 0 else slope)
                w = (OMEGA * mask) / dg
                b = -w * misfit
                base[f, t] = b
                upd[0, f, t, PAD:PAD + E] = b
                gain[f, t] = w * conduct[f]
                mix[f, t] = w * slope * (0.5 if f == 0 else 1.0)
                diag[f, t] = dg * (1.0 / OMEGA)
                pack_z(planes, f, t, b)
                if t == 0:
                    ends[f][0] = b
                if t == TILES - 1:
                    ends[f][1] = b
        post_y(r0 + 1, ends)
        post_z(r0 + 1, planes)
        squares_a[k, 0] = fold(square)
        gather_start(over_a, k, "space", me_s, n)

        def terms(u, t, ghosts):
            pairs = [around(u, f, t, ghosts) for f in range(3)]
            c, e, s = (p[0] for p in pairs)
            half = 0.5 * c
            cross = (s - e, s - half, e + half)
            return [(pairs[f][0], base[f, t] + gain[f, t] * pairs[f][1] + mix[f, t] * cross[f]) for f in range(3)]

        no_y = ([0.0] * 3, [0.0] * 3)

        def y_extras(r):
            lows, highs = ghosts_y(r, False)
            for f in range(3):
                yield f, 0, gain[f, 0] * jnp.where(block == 0, lows[f], 0.0)
                yield f, TILES - 1, gain[f, TILES - 1] * jnp.where(block == 3, highs[f], 0.0)

        def smooth(p, carry):
            now = lax.rem(p, 2)
            u, later = upd.at[now], upd.at[1 - now]
            ghosts = (ghosts_z(r0 + 1 + p, False), no_y)
            parts = {}
            planes, ends = [None, None], [[None, None] for _ in range(3)]
            for t in inside + outside:
                for f, (v, term) in enumerate(terms(u, t, ghosts)):
                    value = (1.0 - OMEGA) * v + term
                    if t in outside:
                        parts[f, t] = value
                    else:
                        later[f, t, PAD:PAD + E] = value
                        pack_z(planes, f, t, value)
            for f, t, extra in y_extras(r0 + 1 + p):
                ends[f][t // (TILES - 1)] = parts[f, t] + extra
            post_y(r0 + 2 + p, ends)
            for f in range(3):
                for t in outside:
                    value = ends[f][t // (TILES - 1)]
                    later[f, t, PAD:PAD + E] = value
                    pack_z(planes, f, t, value)
            post_z(r0 + 2 + p, planes)
            return carry

        lax.fori_loop(0, 1, smooth, 0)
        gather_wait(over_a, k, "space", me_s, n)
        part = squares_a[k, 0]
        for d in range(1, n):
            part = part + squares_a[k, d]
        squares_b[k, 0] = part
        gather_start(over_b, k, "group", me_g, m)
        lax.fori_loop(1, SMOOTH - 1, smooth, 0)

        u = upd.at[(SMOOTH - 1) % 2]
        ghosts = (ghosts_z(r0 + SMOOTH, False), no_y)
        sums = [jnp.zeros((E, 128), F32) for _ in range(3)]
        for t in inside + outside:
            for f, (v, term) in enumerate(terms(u, t, ghosts)):
                sums[f] = sums[f] + diag[f, t] * (term - OMEGA * v)
        for f, t, extra in y_extras(r0 + SMOOTH):
            sums[f] = sums[f] + diag[f, t] * extra
        rows = [jnp.sum(x, axis=0, keepdims=True) for x in sums]
        coarse[k, 0] = jnp.where(rows8 == 0, rows[0], jnp.where(rows8 == 1, rows[1], jnp.where(rows8 == 2, rows[2], 0.0)))
        gather_start(over_c, k, "space", me_s, n)

        gather_wait(over_b, k, "group", me_g, m)
        part = squares_b[k, 0]
        for d in range(1, m):
            part = part + squares_b[k, d]
        whole = jnp.sum(jnp.sum(part, axis=0, keepdims=True), axis=1, keepdims=True)
        cells = 3.0 * n * m * E * E * E
        damping = 1.0 / (1.0 + jnp.sqrt(whole / cells + 1e-6))

        planes, ends = [None, None], []
        for f in range(3):
            tiles = []
            for t in range(TILES):
                value = state[f, t, PAD:PAD + E] + damping * u[f, t, PAD:PAD + E]
                state[f, t, PAD:PAD + E] = value
                pack_z(planes, f, t, value)
                tiles.append(value)
            ends.append((tiles[0], tiles[TILES - 1]))
            for h in range(2):
                got = swap4(tiles[4 * h:4 * h + 4])
                for q in range(4):
                    t = 2 * q + h
                    out[f, :, t * 128:(t + 1) * 128] = got[q]
        pack = y_planes(ends) + z_planes(planes)

        gather_wait(over_c, k, "space", me_s, n)
        got = [coarse[k, d] for d in range(n)]
        lifts = []
        for f in range(3):
            acc = got[0] * weights[f, 0]
            for d in range(1, n):
                acc = acc + got[d] * weights[f, d]
            lifts.append(damping * (mask * jnp.sum(jnp.sum(acc, axis=0, keepdims=True), axis=1, keepdims=True)))

        @pl.when(k < NEWTON - 1)
        def _():
            by_block = jnp.where(block == 0, lifts[0], jnp.where(block == 1, lifts[1], lifts[2]))
            below = jnp.where(even, lifts[2], jnp.where((depth < 15) | last, lifts[0], lifts[1]))
            above = jnp.where(even, jnp.where(depth < 16, lifts[0], lifts[1]), lifts[2])
            for d, part in enumerate((by_block, by_block, below, above)):
                send[r0 + ROUNDS, d] = pack[d] + part
            start_faces(r0 + ROUNDS, (0, 1, 2, 3))
            for f in range(3):
                for t in range(TILES):
                    state[f, t, PAD:PAD + E] = state[f, t, PAD:PAD + E] + lifts[f]

        @pl.when(k == NEWTON - 1)
        def _():
            for f in range(3):
                out[f] = out[f] + lifts[f]

        return carry

    lax.fori_loop(0, NEWTON, sweep, 0)

    for r in range(NEWTON * ROUNDS):
        for d in range(4):
            @pl.when(has(*targets[d]))
            def _():
                face_copy(r, d).wait_send()
    for k in range(NEWTON):
        for bufs, axis, me, size in ((over_a, "space", me_s, n), (over_b, "group", me_g, m), (over_c, "space", me_s, n)):
            for d in range(1, size):
                gather_copy(*bufs, k, d, axis, me, size).wait_send()


def shards(n, m, initial_state, phases, brick_coords, neighbours, source, coarse_inverse):
    rounds = NEWTON * ROUNDS
    anywhere = pl.BlockSpec(memory_space=pl.ANY)
    vmem = pl.BlockSpec(memory_space=pltpu.VMEM)
    padded = (3, TILES, E + 2 * PAD, 128)
    inner = (3, TILES, E, 128)
    dma = pltpu.SemaphoreType.DMA
    result = pl.pallas_call(
        functools.partial(kernel, n, m),
        out_shape=jax.ShapeDtypeStruct((3, E, E * E), F32),
        in_specs=[anywhere] * 6,
        out_specs=vmem,
        scratch_shapes=[
            pltpu.SMEM((1, 3), jnp.int32),
            pltpu.SMEM((1, 6), jnp.int32),
            pltpu.SMEM((3, 1, 3 * n), F32),
            pltpu.VMEM((3, E, E * E), F32),
            pltpu.VMEM((E, E * E), jnp.int32),
            pltpu.VMEM((3, E, E * E), F32),
            dma((6,)),
            pltpu.VMEM(padded, F32),
            pltpu.VMEM((2,) + padded, F32),
            pltpu.VMEM(inner, F32),
            pltpu.VMEM(inner, F32),
            pltpu.VMEM(inner, F32),
            pltpu.VMEM(inner, F32),
            pltpu.VMEM(inner, F32),
            pltpu.VMEM(inner[1:], jnp.int32),
            pltpu.VMEM((rounds, 4, E, 128), F32),
            pltpu.VMEM((rounds, 4, E, 128), F32),
            pltpu.VMEM((NEWTON, n, 8, 128), F32),
            pltpu.VMEM((NEWTON, m, 8, 128), F32),
            pltpu.VMEM((NEWTON, n, 8, 128), F32),
            pltpu.VMEM((3, n, 8, 128), F32),
            dma((rounds, 4)), dma((rounds, 4)),
            dma((NEWTON, n)), dma((NEWTON, n)),
            dma((NEWTON, m)), dma((NEWTON, m)),
            dma((NEWTON, n)), dma((NEWTON, n)),
        ],
        compiler_params=pltpu.CompilerParams(
            collective_id=0, has_side_effects=True, vmem_limit_bytes=56 * 1024 * 1024
        ),
    )(brick_coords, neighbours, jnp.swapaxes(coarse_inverse, 0, 1), initial_state[0], phases[0], source[0])
    return result[None]


def solution(mesh):
    both = ("group", "space")
    return jax.shard_map(
        functools.partial(shards, mesh.shape["space"], mesh.shape["group"]),
        mesh=mesh,
        in_specs=(
            P(both, None, None, None),
            P(both, None, None),
            P(both, None),
            P(both, None),
            P(both, None, None, None),
            P("group", "space", None),
        ),
        out_specs=P(both, None, None, None),
        check_vma=False,
    )
```

profile of v0, /device:TPU:0, one launch (start us, length us, event | category | flops | bytes accessed | tf_op | source)
XLA Modules:
  0.0 52.1 jit_solution(11941513343259416779)
XLA Ops:
  0.0 50.3 %shard_map.64 = f32[3,32,1024]{2,1,0:T(8,128)} custom-call(s32[1,3]{1,0:T(1,128)} %coords_in.1, s32[1,6]{1,0:T(1,128)} %links_in.1, f32[3,1,24]{2,1,0:T(1,128)} %bitcast.9, f32[3,32,1024]{2,1,0:T(8,128)} %bitcast.6, s32[32,1024]{1,0:T(8,128)} %bitcast.8, f32[3,32,1024]{2,1,0:T(8,128)} %bitcast.7), custom_call_target="tpu_custom_call" | custom-call | tf_op jit(solution)/shard_map/pallas_call | solution.py:431
  50.3 1.8 %copy.8 = f32[1,3,32,1024]{3,2,1,0:T(8,128)} copy(f32[1,3,32,1024]{3,2,1,0:T(8,128)} %bitcast.5) | data formatting | bytes 786432
where the time goes:
time: 52.2 us; the launch traced here: 52.1 us
  Pallas kernels  50.3 us (96%)
  local copies, waits for them, and re-layouts  1.77 us (3%)
    pallas_call x1, Pallas kernels, shards(): pl.pallas_call(functools.partial(kernel, n, m), out_shape=jax.ShapeDtypeS...  50.3 us
    unnamed x1, local copies, waits for them, and re-layouts  1.77 us

commit v1 on v0

v1 whole, which is shorter than its diff:
```python
import functools

import jax
import jax.numpy as jnp
from jax import lax
from jax.experimental import pallas as pl
from jax.experimental.pallas import tpu as pltpu
from jax.sharding import PartitionSpec as P

NEWTON = 2
SMOOTH = 4
E = 32
RAW = 8
DEEP = 5
WIDE = E + 2 * DEEP
BLOCKS = 3
TILES = WIDE // BLOCKS
PAD = 8
OMEGA = 0.8
FAR = -1000.0
MESH = pl.DeviceIdType.MESH
F32 = jnp.float32


def roll(x, shift):
    shift = shift % 128
    return x if shift == 0 else pltpu.roll(x, shift, 1)


def spot(y):
    block, tile = divmod(y + DEEP, TILES)
    return tile, WIDE * block + DEEP


def kernel(
    n, m,
    coords_in, inverse_in, state_hbm, phase_hbm, source_hbm, out,
    coords, inverse, state_in, phase_in, source_in, fetch,
    state, upd, gain, mix, diag, source, label, last_u,
    near, y_state, y_source, y_misc_out, y_misc, d_out, d_in, z_out, z_in, in_send, in_recv,
    yu_out, yu_in, du_out, du_in, zu_out, zu_in, u_send, u_recv,
    squares, sq_send, sq_recv, coarse, c_send, c_recv,
):
    me_s = lax.axis_index("space")
    me_g = lax.axis_index("group")
    lane = lax.broadcasted_iota(jnp.int32, (E, 128), 1)
    quarter = lane // 32
    block = jnp.where(lane < WIDE, 0, jnp.where(lane < 2 * WIDE, 1, 2))
    column = lane - WIDE * block
    slot = column // DEEP
    own_columns = (column >= DEEP) & (column < DEEP + E)
    low_columns = column < DEEP
    high_columns = (column >= DEEP + E) & (column < WIDE)
    own_rows = (block != 0, block >= 0, block != 2)
    lane8 = lax.broadcasted_iota(jnp.int32, (8, 128), 1)

    def kind(t):
        return 0 if t < DEEP else (1 if t < TILES - DEEP else 2)

    fetches = [
        pltpu.make_async_copy(a, b, fetch.at[i])
        for i, (a, b) in enumerate((
            (coords_in, coords), (state_hbm, state_in), (phase_hbm, phase_in),
            (source_hbm, source_in), (inverse_in, inverse),
        ))
    ]
    for copy in fetches:
        copy.start()

    def there(ds, dg):
        s, g = me_s + ds, me_g + dg
        return (s >= 0) & (s < n) & (g >= 0) & (g < m)

    def at(ds, dg):
        return {"space": jnp.clip(me_s + ds, 0, n - 1), "group": jnp.clip(me_g + dg, 0, m - 1)}

    barrier = pltpu.get_barrier_semaphore()

    def greet(s, g):
        pl.semaphore_signal(barrier, inc=1, device_id={"space": s, "group": g}, device_id_type=MESH)

    for dg in (-1, 0, 1):
        @pl.when(there(0, dg))
        def _():
            for d in range(1 if dg == 0 else 0, n):
                greet(lax.rem(me_s + d, n), jnp.clip(me_g + dg, 0, m - 1))
    for d in range(2, m - 1):
        @pl.when((lax.rem(me_g + d, m) != me_g - 1) & (lax.rem(me_g + d, m) != me_g + 1))
        def _():
            greet(me_s, lax.rem(me_g + d, m))
    for d in sorted({1, m - 1}):
        other = lax.rem(me_g + d, m)

        @pl.when((other != me_g - 1) & (other != me_g + 1))
        def _():
            greet(me_s, other)
    sides = jnp.where(me_g > 0, 1, 0) + jnp.where(me_g < m - 1, 1, 0)
    greeted = n - 1 + n * sides + (m - 1 - sides)

    def message(src, dst, sems, i, ds, dg):
        return pltpu.make_async_remote_copy(
            src_ref=src, dst_ref=dst, send_sem=sems[0].at[i], recv_sem=sems[1].at[i],
            device_id=at(ds, dg), device_id_type=MESH)

    ins = (in_send, in_recv)
    us = (u_send, u_recv)
    steps = (1, -1)
    first_messages, update_messages = {}, {}
    for side in range(2):
        cut = pl.ds(128 * (RAW - 1), 128) if side == 0 else pl.ds(0, 128)
        step = steps[side]
        first_messages["state", side] = (state_hbm.at[:, :, cut], y_state.at[side], ins, side, step, 0)
        first_messages["source", side] = (source_hbm.at[:, :, cut], y_source.at[side], ins, 2 + side, step, 0)
        first_messages["misc", side] = (y_misc_out.at[side], y_misc.at[side], ins, 4 + side, step, 0)
        first_messages["z", side] = (z_out.at[side], z_in.at[side], ins, 6 + side, 0, step)
        update_messages["y", side] = (yu_out.at[side], yu_in.at[side], us, side, step, 0)
        update_messages["z", side] = (zu_out.at[side], zu_in.at[side], us, 2 + side, 0, step)
        for over in range(2):
            c = 2 * side + over
            first_messages["d", c] = (d_out.at[c], d_in.at[c], ins, 8 + c, step, steps[over])
            update_messages["d", c] = (du_out.at[c], du_in.at[c], us, 4 + c, step, steps[over])

    def start(spec):
        @pl.when(there(spec[4], spec[5]))
        def _():
            message(*spec).start()

    def arrive(spec):
        @pl.when(there(-spec[4], -spec[5]))
        def _():
            message(*spec).wait_recv()

    def left(spec):
        @pl.when(there(spec[4], spec[5]))
        def _():
            message(*spec).wait_send()

    pl.semaphore_wait(barrier, greeted)
    for side in range(2):
        start(first_messages["state", side])
        start(first_messages["source", side])

    fetches[0].wait()
    occupied = coords[0, 0] >= 0
    mask = jnp.where(occupied, 1.0, 0.0).astype(F32)
    place_x = coords[0, 0].astype(F32)
    offset = 4.0 * place_x
    compare = jnp.where(occupied, offset, 1000.0)

    fetches[4].wait()
    near[4] = jnp.zeros((8, 128), F32)
    for f in range(3):
        near[4, f:f + 1, 0:3 * n] = inverse[f]
    mine = near[4]

    fetches[1].wait()
    fetches[2].wait()

    def raw_state(f, t):
        return state_in[f, :, t * 128:(t + 1) * 128]

    def raw_source(f, t):
        return source_in[f, :, t * 128:(t + 1) * 128]

    def raw_label(t):
        return phase_in[:, t * 128:(t + 1) * 128].astype(F32) + offset

    for side in range(2):
        edge, inner, q = ((RAW - 1, RAW - 2, 3), (0, 1, 0))[side]
        y_misc_out[side, 0:E] = raw_label(edge)
        fifth = roll(raw_label(inner), 32 * (3 - q))
        for f in range(3):
            fifth = jnp.where(quarter == f, roll(raw_state(f, inner), 32 * (f - q)), fifth)
        y_misc_out[side, E:2 * E] = fifth
        y_misc_out[side, 2 * E:] = mine
        start(first_messages["misc", side])

    small = (lane % 32) // 4

    def corner_pack(tiles, over):
        out_tile = None
        for a, tile in enumerate(tiles):
            part = roll(tile, 4 * a - (28 if over == 0 else 0))
            out_tile = part if out_tile is None else jnp.where(small == a, part, out_tile)
        return out_tile

    fetches[3].wait()
    for side in range(2):
        edge = (RAW - 1, 0)[side]
        tiles = [raw_state(f, edge) for f in range(3)] + [raw_source(f, edge) for f in range(3)] + [raw_label(edge)]
        for over in range(2):
            c = 2 * side + over
            d_out[c, 0:E] = corner_pack(tiles, over)
            d_out[c, E:] = mine
            start(first_messages["d", c])

    class View:
        def __init__(self, read, write):
            self.read, self.write = read, write

    def padded(ref, f):
        def write(t, v):
            ref[f, t, PAD:PAD + E] = v
        return View(lambda t: ref[f, t, PAD:PAD + E], write)

    def plain(ref, *index):
        def write(t, v):
            ref[(*index, t)] = v
        return View(lambda t: ref[(*index, t)], write)

    views = [padded(state, f) for f in range(3)] + [plain(source, f) for f in range(3)] + [plain(label)]
    raws = [functools.partial(raw_state, f) for f in range(3)] + [functools.partial(raw_source, f) for f in range(3)] + [raw_label]

    zero_rows = jnp.zeros((PAD, 128), F32)
    for t in range(TILES):
        for f in range(3):
            state[f, t, 0:PAD] = zero_rows
            state[f, t, PAD + E:] = zero_rows
            for b in range(SMOOTH - 1):
                upd[b, f, t, 0:PAD] = zero_rows
                upd[b, f, t, PAD + E:] = zero_rows
        for a, (view, raw) in enumerate(zip(views, raws)):
            tile = jnp.full((E, 128), FAR if a == 6 else 0.0, F32)
            for b in range(BLOCKS):
                y = TILES * b + t - DEEP
                if 0 <= y < E:
                    moved = roll(raw(y // 4), WIDE * b + DEEP - 32 * (y % 4))
                    tile = jnp.where(own_columns & (block == b), moved, tile)
            view.write(t, tile)

    half_slots = WIDE // DEEP

    def z_pack(parts, side):
        shift = -(E if side == 0 else DEEP)
        packed = []
        for view in parts:
            for low in (0, half_slots):
                acc = None
                for j in range(min(half_slots, TILES - low)):
                    part = roll(view.read(low + j), DEEP * j + shift)
                    acc = part if acc is None else jnp.where(slot == j, part, acc)
                packed.append(acc)
        return packed

    def z_unpack(parts, got):
        for a, view in enumerate(parts):
            for t in range(TILES):
                half, j = divmod(t, half_slots)
                rows = own_rows[kind(t)]
                tile = jnp.where(low_columns & rows, roll(got(0, 2 * a + half), -DEEP * j), view.read(t))
                view.write(t, jnp.where(high_columns & rows, roll(got(1, 2 * a + half), DEEP + E - DEEP * j), tile))

    def halo_tile(side, q):
        if side == 0:
            return (0 if q < 0 else 1 + q), 0
        return (TILES - 1 if q < 0 else TILES - DEEP + q), 2 * WIDE

    def corner_unpack(parts, got):
        for side in range(2):
            for q in range(4):
                t, first = halo_tile(side, q)
                for a, view in enumerate(parts):
                    tile = view.read(t)
                    for over in range(2):
                        begin = first + (1 if over == 0 else DEEP + E)
                        moved = roll(got(2 * side + over), begin - (32 * q + 4 * a))
                        tile = jnp.where((lane >= begin) & (lane < begin + 4), moved, tile)
                    view.write(t, tile)

    def y_unpack(parts, got, fifth, blocks):
        for side in range(2):
            for q in range(-1, 4):
                t, first = halo_tile(side, q)
                here = (lane >= first + DEEP) & (lane < first + DEEP + E)
                for a, view in enumerate(parts):
                    if q < 0 and blocks[a] is None:
                        continue
                    if q < 0:
                        moved = roll(fifth(side), first + DEEP - 32 * blocks[a])
                    else:
                        moved = roll(got(side, a), first + DEEP - 32 * q)
                    view.write(t, jnp.where(here, moved, view.read(t)))

    for side in range(2):
        for i, tile in enumerate(z_pack(views, side)):
            z_out[side, E * i:E * (i + 1)] = tile
        z_out[side, 14 * E:] = mine
        start(first_messages["z", side])

    far = jnp.full((E, 128), FAR, F32)
    none = jnp.zeros((8, 128), F32)
    blank = jnp.zeros((E, 128), F32)
    for side in range(2):
        @pl.when(jnp.logical_not(there(-steps[side], 0)))
        def _():
            for f in range(3):
                y_state[side, f] = blank
                y_source[side, f] = blank
            for i in range(2):
                y_misc[side, E * i:E * (i + 1)] = far
            y_misc[side, 2 * E:] = none
            for i in range(4):
                yu_in[side, E * i:E * (i + 1)] = blank

        @pl.when(jnp.logical_not(there(0, -steps[side])))
        def _():
            for i in range(14):
                z_in[side, E * i:E * (i + 1)] = far
            z_in[side, 14 * E:] = none
            for i in range(6):
                zu_in[side, E * i:E * (i + 1)] = blank
            for k in range(NEWTON):
                for d in range(n):
                    coarse[k, 2 * side, d] = none

        for over in range(2):
            @pl.when(jnp.logical_not(there(-steps[side], -steps[over])))
            def _():
                d_in[2 * side + over, 0:E] = far
                d_in[2 * side + over, E:] = none
                du_in[2 * side + over] = blank

    for side in range(2):
        arrive(first_messages["z", side])
    z_unpack(views, lambda side, i: z_in[side, E * i:E * (i + 1)])
    for c in range(4):
        arrive(first_messages["d", c])
    corner_unpack(views, lambda c: d_in[c, 0:E])
    for side in range(2):
        for name in ("state", "source", "misc"):
            arrive(first_messages[name, side])

    def y_got(side, a):
        if a < 3:
            return y_state[side, a]
        return y_source[side, a - 3] if a < 6 else y_misc[side, 0:E]

    y_unpack(views, y_got, lambda side: y_misc[side, E:2 * E], (0, 1, 2, None, None, None, 3))

    for side in range(2):
        near[1 + 6 * side] = y_misc[side, 2 * E:]
        near[3 + 2 * side] = z_in[side, 14 * E:]
        for over in range(2):
            near[6 * side + 2 * over] = d_in[2 * side + over, E:]

    def by_region(values, t_kind):
        def row(i):
            return jnp.where(low_columns, values[i][0], jnp.where(own_columns, values[i][1], values[i][2]))
        middle = row(1)
        if t_kind == 0:
            return jnp.where(block == 0, row(0), middle)
        return jnp.where(block == 2, row(2), middle) if t_kind == 2 else middle

    walls = [[place_x + (me_s + i).astype(F32) / n + (me_g + j).astype(F32) / m - 1.0 for j in (-1, 0, 1)] for i in (-1, 0, 1)]
    wall_maps = [by_region(walls, i) for i in range(3)]
    row_index = lax.broadcasted_iota(jnp.int32, (E, 128), 0)
    x_open = jnp.where((row_index == 0) | (row_index == E - 1), 1.0, 0.0).astype(F32)

    def is_valid(rel):
        return (rel >= 0.0) & (rel <= 2.0)

    bricks = [jnp.where(is_valid(label[t, 0:8] - compare), 1.0, 0.0).astype(F32) for t in range(TILES)]
    for t in range(TILES):
        rel = label[t] - compare
        label[t] = rel
        good = is_valid(rel)
        for f in range(3):
            state[f, t, PAD:PAD + E] = jnp.where(good, state[f, t, PAD:PAD + E], 0.0)
        below = bricks[t - 1] if t > 0 else roll(bricks[TILES - 1], WIDE)
        above = bricks[t + 1] if t < TILES - 1 else roll(bricks[0], -WIDE)
        shut = 4.0 - (below + above + roll(bricks[t], 1) + roll(bricks[t], -1))
        missing = jnp.concatenate([shut] * 4, axis=0) + x_open
        solid = jnp.where(rel == 0.0, 0.05, jnp.where(rel == 1.0, 0.5, 1.5))
        source[2, t] = source[2, t] + solid * (wall_maps[kind(t)] * missing)

    def around(ref, f, t):
        c = ref[f, t, PAD:PAD + E]
        total = ref[f, t, PAD - 1:PAD - 1 + E] + ref[f, t, PAD + 1:PAD + 1 + E]
        total = total + (roll(c, 1) + roll(c, -1))
        total = total + (ref[f, t - 1, PAD:PAD + E] if t > 0 else roll(ref[f, TILES - 1, PAD:PAD + E], WIDE))
        total = total + (ref[f, t + 1, PAD:PAD + E] if t < TILES - 1 else roll(ref[f, 0, PAD:PAD + E], -WIDE))
        return c, total

    def fold(x):
        return x[0:8] + x[8:16] + x[16:24] + x[24:32]

    def total_of(x):
        return jnp.sum(jnp.sum(x, axis=0, keepdims=True), axis=1, keepdims=True)

    def square_copy(k, d):
        return pltpu.make_async_remote_copy(
            src_ref=squares.at[k, 0], dst_ref=squares.at[k, d],
            send_sem=sq_send.at[k, d], recv_sem=sq_recv.at[k, d],
            device_id={"group": lax.rem(me_g + d, m)}, device_id_type=MESH)

    def coarse_copy(k, dg, d):
        return pltpu.make_async_remote_copy(
            src_ref=coarse.at[k, 1, me_s], dst_ref=coarse.at[k, 1 - dg, me_s],
            send_sem=c_send.at[k, 1 + dg, d], recv_sem=c_recv.at[k, 1 - dg, me_s],
            device_id={"space": lax.rem(me_s + d, n), "group": jnp.clip(me_g + dg, 0, m - 1)}, device_id_type=MESH)

    def coarse_arrival(k, dg, d):
        who = lax.rem(me_s + d, n)
        return pltpu.make_async_remote_copy(
            src_ref=coarse.at[k, 1 + dg, who], dst_ref=coarse.at[k, 1 + dg, who],
            send_sem=c_send.at[k, 1 + dg, d], recv_sem=c_recv.at[k, 1 + dg, who],
            device_id={"space": lax.rem(me_s + (1 if n > 1 else 0), n)}, device_id_type=MESH)

    def sweep(k, carry):
        square = jnp.zeros((E, 128), F32)
        for t in range(TILES):
            rel = label[t]
            pore = rel == 0.0
            active = rel == 1.0
            good = is_valid(rel)
            mine_here = good & own_columns & own_rows[kind(t)]
            conduct = (jnp.where(pore, 1.0, 0.2), jnp.where(pore, 1.0, 0.1),
                       jnp.where(pore, 0.05, jnp.where(active, 0.5, 1.5)))
            rates = jnp.where(pore, 0.0, jnp.where(active, 0.3, 0.02))
            pairs = [around(state, f, t) for f in range(3)]
            c, e, s = (p[0] for p in pairs)
            eta = s - e - 0.5 * c
            forward = jnp.exp(0.5 * eta)
            backward = jnp.exp(-0.5 * eta)
            current = rates * (forward - backward)
            slope = 0.5 * rates * (forward + backward)
            react = (-0.5 * current, -current, current)
            weight = jnp.where(good, OMEGA, 0.0)
            for f in range(3):
                v, total = pairs[f]
                misfit = 0.5 * v + conduct[f] * (6.0 * v - total) + react[f] - source[f, t]
                square = square + jnp.where(mine_here, misfit * misfit, 0.0)
                dg = 0.5 + 6.0 * conduct[f] + (0.25 * slope if f == 0 else slope)
                w = weight / dg
                upd[0, f, t, PAD:PAD + E] = -w * misfit
                gain[f, t] = w * conduct[f]
                mix[f, t] = w * slope * (0.5 if f == 0 else 1.0)
                diag[f, t] = jnp.where(mine_here, dg * (1.0 / OMEGA), 0.0)
        squares[k, 0] = fold(square)
        for d in range(1, m):
            square_copy(k, d).start()

        def terms(u, t):
            pairs = [around(u, f, t) for f in range(3)]
            c, e, s = (p[0] for p in pairs)
            half = 0.5 * c
            cross = (s - e, s - half, e + half)
            return [(pairs[f][0], upd[0, f, t, PAD:PAD + E] + gain[f, t] * pairs[f][1] + mix[f, t] * cross[f]) for f in range(3)]

        def smooth(p, carry):
            u = upd.at[jnp.where(p == 0, 0, 1 + lax.rem(p + 1, 2))]
            later = upd.at[1 + lax.rem(p, 2)]
            for t in range(TILES):
                for f, (v, term) in enumerate(terms(u, t)):
                    later[f, t, PAD:PAD + E] = (1.0 - OMEGA) * v + term
            return carry

        lax.fori_loop(0, SMOOTH - 1, smooth, 0)
        final = 1 + (SMOOTH - 2) % 2
        u = upd.at[final]
        sums = [jnp.zeros((E, 128), F32) for _ in range(3)]
        for t in range(TILES):
            for f, (v, term) in enumerate(terms(u, t)):
                sums[f] = sums[f] + diag[f, t] * (term - OMEGA * v)
        totals = [total_of(x) for x in sums]
        for d in range(1, m):
            square_copy(k, d).wait_recv()
        part = squares[k, 0]
        for d in range(1, m):
            part = part + squares[k, d]
        packed = jnp.where(lane8 == 127, total_of(part), 0.0)
        for f in range(3):
            packed = jnp.where(lane8 == 3 * me_s + f, totals[f], packed)
        coarse[k, 1, me_s] = packed
        for d in range(1, n):
            coarse_copy(k, 0, d).start()

        u_views = [padded(u, f) for f in range(3)]

        def damping_of(group):
            whole = jnp.sum(jnp.where(lane8 == 127, group, 0.0), axis=1, keepdims=True)[0:1]
            cells = 3.0 * n * m * E * E * E
            return 1.0 / (1.0 + jnp.sqrt(whole / cells + 1e-6))

        def group_sum(i):
            acc = coarse[k, i, 0]
            for d in range(1, n):
                acc = acc + coarse[k, i, d]
            return acc

        @pl.when(k < NEWTON - 1)
        def _():
            for dg in (-1, 1):
                @pl.when(there(0, dg))
                def _():
                    for d in range(n):
                        coarse_copy(k, dg, d).start()
            for side in range(2):
                tiles, fifth = [], None
                for f in range(3):
                    tile = None
                    for q in range(4):
                        t, first = spot(E - 4 + q if side == 0 else q)
                        part = roll(u_views[f].read(t), 32 * q - first)
                        tile = part if tile is None else jnp.where(quarter == q, part, tile)
                    tiles.append(tile)
                    t, first = spot(E - 5 if side == 0 else 4)
                    part = roll(u_views[f].read(t), 32 * f - first)
                    fifth = part if fifth is None else jnp.where(quarter == f, part, fifth)
                for i, tile in enumerate(tiles + [fifth]):
                    yu_out[side, E * i:E * (i + 1)] = tile
                start(update_messages["y", side])
                for over in range(2):
                    du_out[2 * side + over] = corner_pack(tiles, over)
                    start(update_messages["d", 2 * side + over])
            for side in range(2):
                for i, tile in enumerate(z_pack(u_views, side)):
                    zu_out[side, E * i:E * (i + 1)] = tile
                start(update_messages["z", side])
            for side in range(2):
                arrive(update_messages["z", side])
            z_unpack(u_views, lambda side, i: zu_in[side, E * i:E * (i + 1)])
            for c in range(4):
                arrive(update_messages["d", c])
            corner_unpack(u_views, lambda c: du_in[c])
            for side in range(2):
                arrive(update_messages["y", side])
            y_unpack(u_views, lambda side, a: yu_in[side, E * a:E * (a + 1)], lambda side: yu_in[side, 3 * E:], (0, 1, 2))

            for d in range(1, n):
                coarse_arrival(k, 0, d).wait_recv()
            for dg in (-1, 1):
                @pl.when(there(0, dg))
                def _():
                    for d in range(n):
                        coarse_arrival(k, dg, d).wait_recv()
            groups = [group_sum(i) for i in range(3)]
            damping = damping_of(groups[1])
            lifts = [[jnp.sum(near[3 * i + j] * groups[j], axis=1, keepdims=True) for j in range(3)] for i in range(3)]
            maps = [[by_region([[x[f:f + 1] for x in row] for row in lifts], i) for i in range(3)] for f in range(3)]
            for t in range(TILES):
                good = is_valid(label[t])
                for f in range(3):
                    value = state[f, t, PAD:PAD + E] + damping * (u[f, t, PAD:PAD + E] + maps[f][kind(t)])
                    state[f, t, PAD:PAD + E] = jnp.where(good, value, 0.0)

        @pl.when(k == NEWTON - 1)
        def _():
            for f in range(3):
                for i in range(RAW):
                    for view, where in ((padded(state, f), out), (u_views[f], last_u)):
                        tile = None
                        for q in range(4):
                            t, first = spot(4 * i + q)
                            part = roll(view.read(t), 32 * q - first)
                            tile = part if tile is None else jnp.where(quarter == q, part, tile)
                        where[f, :, i * 128:(i + 1) * 128] = tile
            for d in range(1, n):
                coarse_arrival(k, 0, d).wait_recv()
            group = group_sum(1)
            damping = damping_of(group)
            lift = mask * jnp.sum(near[4] * group, axis=1, keepdims=True)
            for f in range(3):
                out[f] = out[f] + damping * (last_u[f] + lift[f:f + 1])

        return carry

    lax.fori_loop(0, NEWTON, sweep, 0)

    for spec in list(first_messages.values()) + list(update_messages.values()):
        left(spec)
    for k in range(NEWTON):
        for d in range(1, m):
            square_copy(k, d).wait_send()
        for d in range(1, n):
            coarse_copy(k, 0, d).wait_send()
    for k in range(NEWTON - 1):
        for dg in (-1, 1):
            @pl.when(there(0, dg))
            def _():
                for d in range(n):
                    coarse_copy(k, dg, d).wait_send()


def shards(n, m, initial_state, phases, brick_coords, neighbours, source, coarse_inverse):
    anywhere = pl.BlockSpec(memory_space=pl.ANY)
    vmem = pl.BlockSpec(memory_space=pltpu.VMEM)
    padded = (3, TILES, E + 2 * PAD, 128)
    inner = (3, TILES, E, 128)
    dma = pltpu.SemaphoreType.DMA
    V = pltpu.VMEM
    result = pl.pallas_call(
        functools.partial(kernel, n, m),
        out_shape=jax.ShapeDtypeStruct((3, E, E * E), F32),
        in_specs=[anywhere] * 5,
        out_specs=vmem,
        scratch_shapes=[
            pltpu.SMEM((1, 3), jnp.int32),
            V((3, 1, 3 * n), F32),
            V((3, E, E * E), F32),
            V((E, E * E), jnp.int32),
            V((3, E, E * E), F32),
            dma((5,)),
            V(padded, F32),
            V((SMOOTH - 1,) + padded, F32),
            V(inner, F32),
            V(inner, F32),
            V(inner, F32),
            V(inner, F32),
            V(inner[1:], F32),
            V((3, E, E * E), F32),
            V((9, 8, 128), F32),
            V((2, 3, E, 128), F32), V((2, 3, E, 128), F32),
            V((2, 2 * E + 8, 128), F32), V((2, 2 * E + 8, 128), F32),
            V((4, E + 8, 128), F32), V((4, E + 8, 128), F32),
            V((2, 14 * E + 8, 128), F32), V((2, 14 * E + 8, 128), F32),
            dma((12,)), dma((12,)),
            V((2, 4 * E, 128), F32), V((2, 4 * E, 128), F32),
            V((4, E, 128), F32), V((4, E, 128), F32),
            V((2, 6 * E, 128), F32), V((2, 6 * E, 128), F32),
            dma((8,)), dma((8,)),
            V((NEWTON, m, 8, 128), F32),
            dma((NEWTON, m)), dma((NEWTON, m)),
            V((NEWTON, 3, n, 8, 128), F32),
            dma((NEWTON, 3, n)), dma((NEWTON, 3, n)),
        ],
        compiler_params=pltpu.CompilerParams(
            collective_id=0, has_side_effects=True, vmem_limit_bytes=56 * 1024 * 1024
        ),
    )(brick_coords, jnp.swapaxes(coarse_inverse, 0, 1), initial_state[0], phases[0], source[0])
    return result[None]


def solution(mesh):
    both = ("group", "space")
    return jax.shard_map(
        functools.partial(shards, mesh.shape["space"], mesh.shape["group"]),
        mesh=mesh,
        in_specs=(
            P(both, None, None, None),
            P(both, None, None),
            P(both, None),
            P(both, None),
            P(both, None, None, None),
            P("group", "space", None),
        ),
        out_specs=P(both, None, None, None),
        check_vma=False,
    )
```

time: 52.2 us -> 38.9 us (0.75)
  Pallas kernels: 50.3 us -> 37 us
    pallas_call x1, Pallas kernels: 50.3 us -> 37 us  [shards(): pl.pallas_call(functools.partial(kernel, n, m), out_shape=jax.ShapeDtypeS...]
where the time goes in v1:
time: 38.9 us; the launch traced here: 38.7 us
  Pallas kernels  37 us (95%)
  local copies, waits for them, and re-layouts  1.77 us (5%)
    pallas_call x1, Pallas kernels, shards(): pl.pallas_call(functools.partial(kernel, n, m), out_shape=jax.ShapeDtypeS...  37 us
    unnamed x1, local copies, waits for them, and re-layouts  1.77 us

profile of v1, /device:TPU:0, one launch (start us, length us, event | category | flops | bytes accessed | tf_op | source)
XLA Modules:
  0.0 38.7 jit_solution(14511532848929191228)
XLA Ops:
  0.0 37.0 %shard_map.55 = f32[3,32,1024]{2,1,0:T(8,128)} custom-call(s32[1,3]{1,0:T(1,128)} %coords_in.1, f32[3,1,24]{2,1,0:T(1,128)} %bitcast.9, f32[3,32,1024]{2,1,0:T(8,128)} %bitcast.6, s32[32,1024]{1,0:T(8,128)} %bitcast.8, f32[3,32,1024]{2,1,0:T(8,128)} %bitcast.7), custom_call_target="tpu_custom_call" | custom-call | tf_op jit(solution)/shard_map/pallas_call | solution.py:592
  37.0 1.8 %copy.7 = f32[1,3,32,1024]{3,2,1,0:T(8,128)} copy(f32[1,3,32,1024]{3,2,1,0:T(8,128)} %bitcast.5) | data formatting | bytes 786432

commit v2 on v1

--- a/solution.py
+++ b/solution.py
@@ -27,6 +27,14 @@
     return x if shift == 0 else pltpu.roll(x, shift, 1)
 
 
+def reaches(n):
+    steps, known = [], 1
+    while known < n - 1:
+        steps.append(known)
+        known *= 2
+    return steps
+
+
 def spot(y):
     block, tile = divmod(y + DEEP, TILES)
     return tile, WIDE * block + DEEP
@@ -39,7 +47,7 @@
     state, upd, gain, mix, diag, source, label, last_u,
     near, y_state, y_source, y_misc_out, y_misc, d_out, d_in, z_out, z_in, in_send, in_recv,
     yu_out, yu_in, du_out, du_in, zu_out, zu_in, u_send, u_recv,
-    squares, sq_send, sq_recv, coarse, c_send, c_recv,
+    squares, sq_send, sq_recv, coarse, c_send, c_recv, ready,
 ):
     me_s = lax.axis_index("space")
     me_g = lax.axis_index("group")
@@ -79,23 +87,35 @@
     def greet(s, g):
         pl.semaphore_signal(barrier, inc=1, device_id={"space": s, "group": g}, device_id_type=MESH)
 
-    for dg in (-1, 0, 1):
-        @pl.when(there(0, dg))
-        def _():
-            for d in range(1 if dg == 0 else 0, n):
-                greet(lax.rem(me_s + d, n), jnp.clip(me_g + dg, 0, m - 1))
-    for d in range(2, m - 1):
-        @pl.when((lax.rem(me_g + d, m) != me_g - 1) & (lax.rem(me_g + d, m) != me_g + 1))
-        def _():
-            greet(me_s, lax.rem(me_g + d, m))
-    for d in sorted({1, m - 1}):
+    for ds in (-1, 0, 1):
+        for dg in (-1, 0, 1):
+            if ds or dg:
+                @pl.when(there(ds, dg))
+                def _():
+                    greet(jnp.clip(me_s + ds, 0, n - 1), jnp.clip(me_g + dg, 0, m - 1))
+    for d in range(1, m):
         other = lax.rem(me_g + d, m)
 
         @pl.when((other != me_g - 1) & (other != me_g + 1))
         def _():
             greet(me_s, other)
-    sides = jnp.where(me_g > 0, 1, 0) + jnp.where(me_g < m - 1, 1, 0)
-    greeted = n - 1 + n * sides + (m - 1 - sides)
+    beside_g = jnp.where(me_g > 0, 1, 0) + jnp.where(me_g < m - 1, 1, 0)
+    beside_s = jnp.where(me_s > 0, 1, 0) + jnp.where(me_s < n - 1, 1, 0)
+    greeted = beside_s * (1 + beside_g) + m - 1
+
+    def tell(i):
+        if i < len(reaches(n)):
+            for side, step in enumerate((reaches(n)[i], -reaches(n)[i])):
+                @pl.when(there(step, 0))
+                def _():
+                    pl.semaphore_signal(ready.at[i, side], inc=1, device_id=at(step, 0), device_id_type=MESH)
+
+    def told(i):
+        for side, step in enumerate((reaches(n)[i], -reaches(n)[i])):
+            @pl.when(there(-step, 0))
+            def _():
+                pl.semaphore_wait(ready.at[i, side], 1)
+        tell(i + 1)
 
     def message(src, dst, sems, i, ds, dg):
         return pltpu.make_async_remote_copy(
@@ -135,11 +155,6 @@
         def _():
             message(*spec).wait_send()
 
-    pl.semaphore_wait(barrier, greeted)
-    for side in range(2):
-        start(first_messages["state", side])
-        start(first_messages["source", side])
-
     fetches[0].wait()
     occupied = coords[0, 0] >= 0
     mask = jnp.where(occupied, 1.0, 0.0).astype(F32)
@@ -173,7 +188,6 @@
             fifth = jnp.where(quarter == f, roll(raw_state(f, inner), 32 * (f - q)), fifth)
         y_misc_out[side, E:2 * E] = fifth
         y_misc_out[side, 2 * E:] = mine
-        start(first_messages["misc", side])
 
     small = (lane % 32) // 4
 
@@ -192,7 +206,6 @@
             c = 2 * side + over
             d_out[c, 0:E] = corner_pack(tiles, over)
             d_out[c, E:] = mine
-            start(first_messages["d", c])
 
     class View:
         def __init__(self, read, write):
@@ -285,7 +298,6 @@
         for i, tile in enumerate(z_pack(views, side)):
             z_out[side, E * i:E * (i + 1)] = tile
         z_out[side, 14 * E:] = mine
-        start(first_messages["z", side])
 
     far = jnp.full((E, 128), FAR, F32)
     none = jnp.zeros((8, 128), F32)
@@ -320,6 +332,14 @@
                 d_in[2 * side + over, E:] = none
                 du_in[2 * side + over] = blank
 
+    pl.semaphore_wait(barrier, greeted)
+    tell(0)
+    for c in range(4):
+        start(first_messages["d", c])
+    for name in ("misc", "state", "source", "z"):
+        for side in range(2):
+            start(first_messages[name, side])
+
     for side in range(2):
         arrive(first_messages["z", side])
     z_unpack(views, lambda side, i: z_in[side, E * i:E * (i + 1)])
@@ -329,6 +349,10 @@
     for side in range(2):
         for name in ("state", "source", "misc"):
             arrive(first_messages[name, side])
+
+    steps_told = len(reaches(n))
+    for i in range(min(1, steps_told)):
+        told(i)
 
     def y_got(side, a):
         if a < 3:
@@ -372,6 +396,9 @@
         missing = jnp.concatenate([shut] * 4, axis=0) + x_open
         solid = jnp.where(rel == 0.0, 0.05, jnp.where(rel == 1.0, 0.5, 1.5))
         source[2, t] = source[2, t] + solid * (wall_maps[kind(t)] * missing)
+
+    for i in range(1, steps_told - 2):
+        told(i)
 
     def around(ref, f, t):
         c = ref[f, t, PAD:PAD + E]
@@ -436,6 +463,11 @@
                 gain[f, t] = w * conduct[f]
                 mix[f, t] = w * slope * (0.5 if f == 0 else 1.0)
                 diag[f, t] = jnp.where(mine_here, dg * (1.0 / OMEGA), 0.0)
+        @pl.when(k == 0)
+        def _():
+            for i in range(max(1, steps_told - 2), steps_told - 1):
+                told(i)
+
         squares[k, 0] = fold(square)
         for d in range(1, m):
             square_copy(k, d).start()
@@ -458,43 +490,10 @@
         lax.fori_loop(0, SMOOTH - 1, smooth, 0)
         final = 1 + (SMOOTH - 2) % 2
         u = upd.at[final]
-        sums = [jnp.zeros((E, 128), F32) for _ in range(3)]
-        for t in range(TILES):
-            for f, (v, term) in enumerate(terms(u, t)):
-                sums[f] = sums[f] + diag[f, t] * (term - OMEGA * v)
-        totals = [total_of(x) for x in sums]
-        for d in range(1, m):
-            square_copy(k, d).wait_recv()
-        part = squares[k, 0]
-        for d in range(1, m):
-            part = part + squares[k, d]
-        packed = jnp.where(lane8 == 127, total_of(part), 0.0)
-        for f in range(3):
-            packed = jnp.where(lane8 == 3 * me_s + f, totals[f], packed)
-        coarse[k, 1, me_s] = packed
-        for d in range(1, n):
-            coarse_copy(k, 0, d).start()
-
         u_views = [padded(u, f) for f in range(3)]
 
-        def damping_of(group):
-            whole = jnp.sum(jnp.where(lane8 == 127, group, 0.0), axis=1, keepdims=True)[0:1]
-            cells = 3.0 * n * m * E * E * E
-            return 1.0 / (1.0 + jnp.sqrt(whole / cells + 1e-6))
-
-        def group_sum(i):
-            acc = coarse[k, i, 0]
-            for d in range(1, n):
-                acc = acc + coarse[k, i, d]
-            return acc
-
         @pl.when(k < NEWTON - 1)
         def _():
-            for dg in (-1, 1):
-                @pl.when(there(0, dg))
-                def _():
-                    for d in range(n):
-                        coarse_copy(k, dg, d).start()
             for side in range(2):
                 tiles, fifth = [], None
                 for f in range(3):
@@ -513,6 +512,48 @@
                 for over in range(2):
                     du_out[2 * side + over] = corner_pack(tiles, over)
                     start(update_messages["d", 2 * side + over])
+
+        sums = [jnp.zeros((E, 128), F32) for _ in range(3)]
+        for t in range(TILES):
+            for f, (v, term) in enumerate(terms(u, t)):
+                sums[f] = sums[f] + diag[f, t] * (term - OMEGA * v)
+        totals = [total_of(x) for x in sums]
+        for d in range(1, m):
+            square_copy(k, d).wait_recv()
+        part = squares[k, 0]
+        for d in range(1, m):
+            part = part + squares[k, d]
+        packed = jnp.where(lane8 == 127, total_of(part), 0.0)
+        for f in range(3):
+            packed = jnp.where(lane8 == 3 * me_s + f, totals[f], packed)
+        coarse[k, 1, me_s] = packed
+
+        @pl.when(k == 0)
+        def _():
+            for i in range(max(1, steps_told - 1), steps_told):
+                told(i)
+
+        for d in range(1, n):
+            coarse_copy(k, 0, d).start()
+
+        def damping_of(group):
+            whole = jnp.sum(jnp.where(lane8 == 127, group, 0.0), axis=1, keepdims=True)[0:1]
+            cells = 3.0 * n * m * E * E * E
+            return 1.0 / (1.0 + jnp.sqrt(whole / cells + 1e-6))
+
+        def group_sum(i):
+            acc = coarse[k, i, 0]
+            for d in range(1, n):
+                acc = acc + coarse[k, i, d]
+            return acc
+
+        @pl.when(k < NEWTON - 1)
+        def _():
+            for dg in (-1, 1):
+                @pl.when(there(0, dg))
+                def _():
+                    for d in range(n):
+                        coarse_copy(k, dg, d).start()
             for side in range(2):
                 for i, tile in enumerate(z_pack(u_views, side)):
                     zu_out[side, E * i:E * (i + 1)] = tile
@@ -591,7 +632,7 @@
     V = pltpu.VMEM
     result = pl.pallas_call(
         functools.partial(kernel, n, m),
-        out_shape=jax.ShapeDtypeStruct((3, E, E * E), F32),
+        out_shape=V((3, E, E * E), F32),
         in_specs=[anywhere] * 5,
         out_specs=vmem,
         scratch_shapes=[
@@ -623,6 +664,7 @@
             dma((NEWTON, m)), dma((NEWTON, m)),
             V((NEWTON, 3, n, 8, 128), F32),
             dma((NEWTON, 3, n)), dma((NEWTON, 3, n)),
+            pltpu.SemaphoreType.REGULAR((max(1, len(reaches(n))), 2)),
         ],
         compiler_params=pltpu.CompilerParams(
             collective_id=0, has_side_effects=True, vmem_limit_bytes=56 * 1024 * 1024

time: 38.9 us -> 35.6 us (0.915)
  Pallas kernels: 37 us -> 34.7 us
  local copies, waits for them, and re-layouts: 1.77 us -> 0.75 us
    pallas_call x1, Pallas kernels: 37 us -> 34.7 us  [shards(): pl.pallas_call(functools.partial(kernel, n, m), out_shape=V((3, E, E * E)...]
    unnamed x1, local copies, waits for them, and re-layouts: 1.77 us -> 0.75 us
where the time goes in v2:
time: 35.6 us; the launch traced here: 35.4 us
  Pallas kernels  34.7 us (97%)
  local copies, waits for them, and re-layouts  0.75 us (2%)
    pallas_call x1, Pallas kernels, shards(): pl.pallas_call(functools.partial(kernel, n, m), out_shape=V((3, E, E * E)...  34.7 us
    unnamed x1, local copies, waits for them, and re-layouts  0.75 us

profile of v2, /device:TPU:0, one launch (start us, length us, event | category | flops | bytes accessed | tf_op | source)
XLA Modules:
  0.0 35.4 jit_solution(1411434487840667228)
XLA Ops:
  0.0 34.7 %shard_map.55 = f32[3,32,1024]{2,1,0:T(8,128)S(1)} custom-call(s32[1,3]{1,0:T(1,128)} %coords_in.1, f32[3,1,24]{2,1,0:T(1,128)} %bitcast.9, f32[3,32,1024]{2,1,0:T(8,128)} %bitcast.6, s32[32,1024]{1,0:T(8,128)} %bitcast.8, f32[3,32,1024]{2,1,0:T(8,128)} %bitcast.7), custom_call_target="tpu_custom_call" | custom-call | tf_op jit(solution)/shard_map/pallas_call | solution.py:633
  34.7 0.7 %copy.7 = f32[1,3,32,1024]{3,2,1,0:T(8,128)} copy(f32[1,3,32,1024]{3,2,1,0:T(8,128)S(1)} %bitcast.5) | data formatting | bytes 786432

commit v3 on v2

--- a/solution.py
+++ b/solution.py
@@ -44,8 +44,8 @@
     n, m,
     coords_in, inverse_in, state_hbm, phase_hbm, source_hbm, out,
     coords, inverse, state_in, phase_in, source_in, fetch,
-    state, upd, gain, mix, diag, source, label, last_u,
-    near, y_state, y_source, y_misc_out, y_misc, d_out, d_in, z_out, z_in, in_send, in_recv,
+    state, upd, gain, mix, diag, scale, source, label, last_u,
+    near, y_state, y_source, y_misc_out, y_misc, d_out, d_in, z_out, z_in, zs_out, zs_in, in_send, in_recv,
     yu_out, yu_in, du_out, du_in, zu_out, zu_in, u_send, u_recv,
     squares, sq_send, sq_recv, coarse, c_send, c_recv, ready,
 ):
@@ -133,6 +133,7 @@
         first_messages["source", side] = (source_hbm.at[:, :, cut], y_source.at[side], ins, 2 + side, step, 0)
         first_messages["misc", side] = (y_misc_out.at[side], y_misc.at[side], ins, 4 + side, step, 0)
         first_messages["z", side] = (z_out.at[side], z_in.at[side], ins, 6 + side, 0, step)
+        first_messages["zs", side] = (zs_out.at[side], zs_in.at[side], ins, 12 + side, 0, step)
         update_messages["y", side] = (yu_out.at[side], yu_in.at[side], us, side, step, 0)
         update_messages["z", side] = (zu_out.at[side], zu_in.at[side], us, 2 + side, 0, step)
         for over in range(2):
@@ -201,7 +202,7 @@
     fetches[3].wait()
     for side in range(2):
         edge = (RAW - 1, 0)[side]
-        tiles = [raw_state(f, edge) for f in range(3)] + [raw_source(f, edge) for f in range(3)] + [raw_label(edge)]
+        tiles = [raw_state(f, edge) for f in range(3)] + [raw_label(edge)] + [raw_source(f, edge) for f in range(3)]
         for over in range(2):
             c = 2 * side + over
             d_out[c, 0:E] = corner_pack(tiles, over)
@@ -221,8 +222,8 @@
             ref[(*index, t)] = v
         return View(lambda t: ref[(*index, t)], write)
 
-    views = [padded(state, f) for f in range(3)] + [plain(source, f) for f in range(3)] + [plain(label)]
-    raws = [functools.partial(raw_state, f) for f in range(3)] + [functools.partial(raw_source, f) for f in range(3)] + [raw_label]
+    views = [padded(state, f) for f in range(3)] + [plain(label)] + [plain(source, f) for f in range(3)]
+    raws = [functools.partial(raw_state, f) for f in range(3)] + [raw_label] + [functools.partial(raw_source, f) for f in range(3)]
 
     zero_rows = jnp.zeros((PAD, 128), F32)
     for t in range(TILES):
@@ -233,7 +234,7 @@
                 upd[b, f, t, 0:PAD] = zero_rows
                 upd[b, f, t, PAD + E:] = zero_rows
         for a, (view, raw) in enumerate(zip(views, raws)):
-            tile = jnp.full((E, 128), FAR if a == 6 else 0.0, F32)
+            tile = jnp.full((E, 128), FAR if a == 3 else 0.0, F32)
             for b in range(BLOCKS):
                 y = TILES * b + t - DEEP
                 if 0 <= y < E:
@@ -295,9 +296,11 @@
                     view.write(t, jnp.where(here, moved, view.read(t)))
 
     for side in range(2):
-        for i, tile in enumerate(z_pack(views, side)):
+        for i, tile in enumerate(z_pack(views[:4], side)):
             z_out[side, E * i:E * (i + 1)] = tile
-        z_out[side, 14 * E:] = mine
+        z_out[side, 8 * E:] = mine
+        for i, tile in enumerate(z_pack(views[4:], side)):
+            zs_out[side, E * i:E * (i + 1)] = tile
 
     far = jnp.full((E, 128), FAR, F32)
     none = jnp.zeros((8, 128), F32)
@@ -316,10 +319,11 @@
 
         @pl.when(jnp.logical_not(there(0, -steps[side])))
         def _():
-            for i in range(14):
+            for i in range(8):
                 z_in[side, E * i:E * (i + 1)] = far
-            z_in[side, 14 * E:] = none
+            z_in[side, 8 * E:] = none
             for i in range(6):
+                zs_in[side, E * i:E * (i + 1)] = blank
                 zu_in[side, E * i:E * (i + 1)] = blank
             for k in range(NEWTON):
                 for d in range(n):
@@ -336,34 +340,34 @@
     tell(0)
     for c in range(4):
         start(first_messages["d", c])
-    for name in ("misc", "state", "source", "z"):
+    for name in ("misc", "state", "z", "zs"):
         for side in range(2):
             start(first_messages[name, side])
 
     for side in range(2):
         arrive(first_messages["z", side])
-    z_unpack(views, lambda side, i: z_in[side, E * i:E * (i + 1)])
+    for side in range(2):
+        start(first_messages["source", side])
+    z_unpack(views[:4], lambda side, i: z_in[side, E * i:E * (i + 1)])
+    for side in range(2):
+        arrive(first_messages["zs", side])
+    z_unpack(views[4:], lambda side, i: zs_in[side, E * i:E * (i + 1)])
     for c in range(4):
         arrive(first_messages["d", c])
     corner_unpack(views, lambda c: d_in[c, 0:E])
     for side in range(2):
-        for name in ("state", "source", "misc"):
+        for name in ("state", "misc"):
             arrive(first_messages[name, side])
 
     steps_told = len(reaches(n))
     for i in range(min(1, steps_told)):
         told(i)
 
-    def y_got(side, a):
-        if a < 3:
-            return y_state[side, a]
-        return y_source[side, a - 3] if a < 6 else y_misc[side, 0:E]
-
-    y_unpack(views, y_got, lambda side: y_misc[side, E:2 * E], (0, 1, 2, None, None, None, 3))
+    y_unpack(views[:4], lambda side, a: y_state[side, a] if a < 3 else y_misc[side, 0:E], lambda side: y_misc[side, E:2 * E], (0, 1, 2, 3))
 
     for side in range(2):
         near[1 + 6 * side] = y_misc[side, 2 * E:]
-        near[3 + 2 * side] = z_in[side, 14 * E:]
+        near[3 + 2 * side] = z_in[side, 8 * E:]
         for over in range(2):
             near[6 * side + 2 * over] = d_in[2 * side + over, E:]
 
@@ -400,12 +404,15 @@
     for i in range(1, steps_told - 2):
         told(i)
 
-    def around(ref, f, t):
-        c = ref[f, t, PAD:PAD + E]
+    def tiles_of(ref):
+        return [[ref[f, t, PAD:PAD + E] for t in range(TILES)] for f in range(3)]
+
+    def around(ref, tiles, f, t):
+        c = tiles[f][t]
         total = ref[f, t, PAD - 1:PAD - 1 + E] + ref[f, t, PAD + 1:PAD + 1 + E]
         total = total + (roll(c, 1) + roll(c, -1))
-        total = total + (ref[f, t - 1, PAD:PAD + E] if t > 0 else roll(ref[f, TILES - 1, PAD:PAD + E], WIDE))
-        total = total + (ref[f, t + 1, PAD:PAD + E] if t < TILES - 1 else roll(ref[f, 0, PAD:PAD + E], -WIDE))
+        total = total + (tiles[f][t - 1] if t > 0 else roll(tiles[f][TILES - 1], WIDE))
+        total = total + (tiles[f][t + 1] if t < TILES - 1 else roll(tiles[f][0], -WIDE))
         return c, total
 
     def fold(x):
@@ -435,6 +442,7 @@
 
     def sweep(k, carry):
         square = jnp.zeros((E, 128), F32)
+        tiles = tiles_of(state)
         for t in range(TILES):
             rel = label[t]
             pore = rel == 0.0
@@ -444,7 +452,7 @@
             conduct = (jnp.where(pore, 1.0, 0.2), jnp.where(pore, 1.0, 0.1),
                        jnp.where(pore, 0.05, jnp.where(active, 0.5, 1.5)))
             rates = jnp.where(pore, 0.0, jnp.where(active, 0.3, 0.02))
-            pairs = [around(state, f, t) for f in range(3)]
+            pairs = [around(state, tiles, f, t) for f in range(3)]
             c, e, s = (p[0] for p in pairs)
             eta = s - e - 0.5 * c
             forward = jnp.exp(0.5 * eta)
@@ -459,21 +467,33 @@
                 square = square + jnp.where(mine_here, misfit * misfit, 0.0)
                 dg = 0.5 + 6.0 * conduct[f] + (0.25 * slope if f == 0 else slope)
                 w = weight / dg
+                if kind(t) != 1:
+                    scale[f, t] = w
                 upd[0, f, t, PAD:PAD + E] = -w * misfit
                 gain[f, t] = w * conduct[f]
                 mix[f, t] = w * slope * (0.5 if f == 0 else 1.0)
                 diag[f, t] = jnp.where(mine_here, dg * (1.0 / OMEGA), 0.0)
-        @pl.when(k == 0)
-        def _():
-            for i in range(max(1, steps_told - 2), steps_told - 1):
-                told(i)
-
         squares[k, 0] = fold(square)
         for d in range(1, m):
             square_copy(k, d).start()
 
-        def terms(u, t):
-            pairs = [around(u, f, t) for f in range(3)]
+        @pl.when(k == 0)
+        def _():
+            for i in range(max(1, steps_told - 2), steps_told - 1):
+                told(i)
+            for side in range(2):
+                arrive(first_messages["source", side])
+            for side in range(2):
+                for q in range(4):
+                    t, first = halo_tile(side, q)
+                    here = (lane >= first + DEEP) & (lane < first + DEEP + E)
+                    for f in range(3):
+                        late = jnp.where(here, roll(y_source[side, f], first + DEEP - 32 * q), 0.0)
+                        source[f, t] = source[f, t] + late
+                        upd[0, f, t, PAD:PAD + E] = upd[0, f, t, PAD:PAD + E] + scale[f, t] * late
+
+        def terms(u, tiles, t):
+            pairs = [around(u, tiles, f, t) for f in range(3)]
             c, e, s = (p[0] for p in pairs)
             half = 0.5 * c
             cross = (s - e, s - half, e + half)
@@ -482,8 +502,9 @@
         def smooth(p, carry):
             u = upd.at[jnp.where(p == 0, 0, 1 + lax.rem(p + 1, 2))]
             later = upd.at[1 + lax.rem(p, 2)]
+            tiles = tiles_of(u)
             for t in range(TILES):
-                for f, (v, term) in enumerate(terms(u, t)):
+                for f, (v, term) in enumerate(terms(u, tiles, t)):
                     later[f, t, PAD:PAD + E] = (1.0 - OMEGA) * v + term
             return carry
 
@@ -514,8 +535,9 @@
                     start(update_messages["d", 2 * side + over])
 
         sums = [jnp.zeros((E, 128), F32) for _ in range(3)]
+        tiles = tiles_of(u)
         for t in range(TILES):
-            for f, (v, term) in enumerate(terms(u, t)):
+            for f, (v, term) in enumerate(terms(u, tiles, t)):
                 sums[f] = sums[f] + diag[f, t] * (term - OMEGA * v)
         totals = [total_of(x) for x in sums]
         for d in range(1, m):
@@ -648,14 +670,16 @@
             V(inner, F32),
             V(inner, F32),
             V(inner, F32),
+            V(inner, F32),
             V(inner[1:], F32),
             V((3, E, E * E), F32),
             V((9, 8, 128), F32),
             V((2, 3, E, 128), F32), V((2, 3, E, 128), F32),
             V((2, 2 * E + 8, 128), F32), V((2, 2 * E + 8, 128), F32),
             V((4, E + 8, 128), F32), V((4, E + 8, 128), F32),
-            V((2, 14 * E + 8, 128), F32), V((2, 14 * E + 8, 128), F32),
-            dma((12,)), dma((12,)),
+            V((2, 8 * E + 8, 128), F32), V((2, 8 * E + 8, 128), F32),
+            V((2, 6 * E, 128), F32), V((2, 6 * E, 128), F32),
+            dma((14,)), dma((14,)),
             V((2, 4 * E, 128), F32), V((2, 4 * E, 128), F32),
             V((4, E, 128), F32), V((4, E, 128), F32),
             V((2, 6 * E, 128), F32), V((2, 6 * E, 128), F32),

time: 35.6 us -> 34.5 us (0.969)
  Pallas kernels: 34.7 us -> 33.6 us
    pallas_call x1, Pallas kernels: 34.7 us -> 33.6 us  [shards(): pl.pallas_call(functools.partial(kernel, n, m), out_shape=V((3, E, E * E)...]
where the time goes in v3:
time: 34.5 us; the launch traced here: 34.4 us
  Pallas kernels  33.6 us (97%)
  local copies, waits for them, and re-layouts  0.75 us (2%)
    pallas_call x1, Pallas kernels, shards(): pl.pallas_call(functools.partial(kernel, n, m), out_shape=V((3, E, E * E)...  33.6 us
    unnamed x1, local copies, waits for them, and re-layouts  0.75 us

profile of v3, /device:TPU:0, one launch (start us, length us, event | category | flops | bytes accessed | tf_op | source)
XLA Modules:
  0.0 34.4 jit_solution(9708106117046477671)
XLA Ops:
  0.0 33.6 %shard_map.55 = f32[3,32,1024]{2,1,0:T(8,128)S(1)} custom-call(s32[1,3]{1,0:T(1,128)} %coords_in.1, f32[3,1,24]{2,1,0:T(1,128)} %bitcast.9, f32[3,32,1024]{2,1,0:T(8,128)} %bitcast.6, s32[32,1024]{1,0:T(8,128)} %bitcast.8, f32[3,32,1024]{2,1,0:T(8,128)} %bitcast.7), custom_call_target="tpu_custom_call" | custom-call | tf_op jit(solution)/shard_map/pallas_call | solution.py:655
  33.6 0.7 %copy.7 = f32[1,3,32,1024]{3,2,1,0:T(8,128)} copy(f32[1,3,32,1024]{3,2,1,0:T(8,128)S(1)} %bitcast.5) | data formatting | bytes 786432

commit v4 on v3

--- a/solution.py
+++ b/solution.py
@@ -164,10 +164,10 @@
     compare = jnp.where(occupied, offset, 1000.0)
 
     fetches[4].wait()
-    near[4] = jnp.zeros((8, 128), F32)
+    near[...] = jnp.zeros((8, 128), F32)
     for f in range(3):
-        near[4, f:f + 1, 0:3 * n] = inverse[f]
-    mine = near[4]
+        near[f:f + 1, 0:3 * n] = inverse[f]
+    mine = near[...]
 
     fetches[1].wait()
     fetches[2].wait()
@@ -188,7 +188,7 @@
         for f in range(3):
             fifth = jnp.where(quarter == f, roll(raw_state(f, inner), 32 * (f - q)), fifth)
         y_misc_out[side, E:2 * E] = fifth
-        y_misc_out[side, 2 * E:] = mine
+        yu_out[side, 3 * E:] = mine
 
     small = (lane % 32) // 4
 
@@ -205,8 +205,8 @@
         tiles = [raw_state(f, edge) for f in range(3)] + [raw_label(edge)] + [raw_source(f, edge) for f in range(3)]
         for over in range(2):
             c = 2 * side + over
-            d_out[c, 0:E] = corner_pack(tiles, over)
-            d_out[c, E:] = mine
+            d_out[c] = corner_pack(tiles, over)
+            du_out[c, E:] = mine
 
     class View:
         def __init__(self, read, write):
@@ -298,7 +298,7 @@
     for side in range(2):
         for i, tile in enumerate(z_pack(views[:4], side)):
             z_out[side, E * i:E * (i + 1)] = tile
-        z_out[side, 8 * E:] = mine
+        zu_out[side, 6 * E:] = mine
         for i, tile in enumerate(z_pack(views[4:], side)):
             zs_out[side, E * i:E * (i + 1)] = tile
 
@@ -313,15 +313,15 @@
                 y_source[side, f] = blank
             for i in range(2):
                 y_misc[side, E * i:E * (i + 1)] = far
-            y_misc[side, 2 * E:] = none
-            for i in range(4):
+            yu_in[side, 3 * E:] = none
+            for i in range(3):
                 yu_in[side, E * i:E * (i + 1)] = blank
 
         @pl.when(jnp.logical_not(there(0, -steps[side])))
         def _():
             for i in range(8):
                 z_in[side, E * i:E * (i + 1)] = far
-            z_in[side, 8 * E:] = none
+            zu_in[side, 6 * E:] = none
             for i in range(6):
                 zs_in[side, E * i:E * (i + 1)] = blank
                 zu_in[side, E * i:E * (i + 1)] = blank
@@ -332,9 +332,9 @@
         for over in range(2):
             @pl.when(jnp.logical_not(there(-steps[side], -steps[over])))
             def _():
-                d_in[2 * side + over, 0:E] = far
-                d_in[2 * side + over, E:] = none
-                du_in[2 * side + over] = blank
+                d_in[2 * side + over] = far
+                du_in[2 * side + over, 0:E] = blank
+                du_in[2 * side + over, E:] = none
 
     pl.semaphore_wait(barrier, greeted)
     tell(0)
@@ -354,7 +354,7 @@
     z_unpack(views[4:], lambda side, i: zs_in[side, E * i:E * (i + 1)])
     for c in range(4):
         arrive(first_messages["d", c])
-    corner_unpack(views, lambda c: d_in[c, 0:E])
+    corner_unpack(views, lambda c: d_in[c])
     for side in range(2):
         for name in ("state", "misc"):
             arrive(first_messages[name, side])
@@ -364,12 +364,6 @@
         told(i)
 
     y_unpack(views[:4], lambda side, a: y_state[side, a] if a < 3 else y_misc[side, 0:E], lambda side: y_misc[side, E:2 * E], (0, 1, 2, 3))
-
-    for side in range(2):
-        near[1 + 6 * side] = y_misc[side, 2 * E:]
-        near[3 + 2 * side] = z_in[side, 8 * E:]
-        for over in range(2):
-            near[6 * side + 2 * over] = d_in[2 * side + over, E:]
 
     def by_region(values, t_kind):
         def row(i):
@@ -499,41 +493,44 @@
             cross = (s - e, s - half, e + half)
             return [(pairs[f][0], upd[0, f, t, PAD:PAD + E] + gain[f, t] * pairs[f][1] + mix[f, t] * cross[f]) for f in range(3)]
 
-        def smooth(p, carry):
-            u = upd.at[jnp.where(p == 0, 0, 1 + lax.rem(p + 1, 2))]
-            later = upd.at[1 + lax.rem(p, 2)]
+        def smooth_tiles(u, later, which):
             tiles = tiles_of(u)
-            for t in range(TILES):
+            for t in which:
                 for f, (v, term) in enumerate(terms(u, tiles, t)):
                     later[f, t, PAD:PAD + E] = (1.0 - OMEGA) * v + term
+
+        def smooth(p, carry):
+            smooth_tiles(upd.at[jnp.where(p == 0, 0, 1 + lax.rem(p + 1, 2))], upd.at[1 + lax.rem(p, 2)], range(TILES))
             return carry
 
-        lax.fori_loop(0, SMOOTH - 1, smooth, 0)
-        final = 1 + (SMOOTH - 2) % 2
-        u = upd.at[final]
+        lax.fori_loop(0, SMOOTH - 2, smooth, 0)
+        u_last = upd.at[1 + (SMOOTH - 3) % 2]
+        u = upd.at[1 + (SMOOTH - 2) % 2]
         u_views = [padded(u, f) for f in range(3)]
+        sent_rows = range(DEEP - 1, TILES - DEEP + 1)
+        smooth_tiles(u_last, u, sent_rows)
 
         @pl.when(k < NEWTON - 1)
         def _():
             for side in range(2):
-                tiles, fifth = [], None
+                corner_tiles = []
                 for f in range(3):
                     tile = None
                     for q in range(4):
                         t, first = spot(E - 4 + q if side == 0 else q)
                         part = roll(u_views[f].read(t), 32 * q - first)
                         tile = part if tile is None else jnp.where(quarter == q, part, tile)
-                    tiles.append(tile)
+                    corner_tiles.append(tile)
                     t, first = spot(E - 5 if side == 0 else 4)
-                    part = roll(u_views[f].read(t), 32 * f - first)
-                    fifth = part if fifth is None else jnp.where(quarter == f, part, fifth)
-                for i, tile in enumerate(tiles + [fifth]):
-                    yu_out[side, E * i:E * (i + 1)] = tile
+                    q = (0, 3)[side]
+                    deepest = roll(u_views[f].read(t), 32 * q - first)
+                    yu_out[side, E * f:E * (f + 1)] = jnp.where(quarter == q, deepest, roll(tile, (32, -32)[side]))
                 start(update_messages["y", side])
                 for over in range(2):
-                    du_out[2 * side + over] = corner_pack(tiles, over)
+                    du_out[2 * side + over, 0:E] = corner_pack(corner_tiles, over)
                     start(update_messages["d", 2 * side + over])
 
+        smooth_tiles(u_last, u, [t for t in range(TILES) if t not in sent_rows])
         sums = [jnp.zeros((E, 128), F32) for _ in range(3)]
         tiles = tiles_of(u)
         for t in range(TILES):
@@ -585,10 +582,16 @@
             z_unpack(u_views, lambda side, i: zu_in[side, E * i:E * (i + 1)])
             for c in range(4):
                 arrive(update_messages["d", c])
-            corner_unpack(u_views, lambda c: du_in[c])
+            corner_unpack(u_views, lambda c: du_in[c, 0:E])
             for side in range(2):
                 arrive(update_messages["y", side])
-            y_unpack(u_views, lambda side, a: yu_in[side, E * a:E * (a + 1)], lambda side: yu_in[side, 3 * E:], (0, 1, 2))
+            for side in range(2):
+                for q in range(4):
+                    t, first = (q, 0) if side == 0 else (TILES - 4 + q, 2 * WIDE)
+                    here = (lane >= first + DEEP) & (lane < first + DEEP + E)
+                    for f in range(3):
+                        moved = roll(yu_in[side, E * f:E * (f + 1)], first + DEEP - 32 * q)
+                        u[f, t, PAD:PAD + E] = jnp.where(here, moved, u[f, t, PAD:PAD + E])
 
             for d in range(1, n):
                 coarse_arrival(k, 0, d).wait_recv()
@@ -599,7 +602,14 @@
                         coarse_arrival(k, dg, d).wait_recv()
             groups = [group_sum(i) for i in range(3)]
             damping = damping_of(groups[1])
-            lifts = [[jnp.sum(near[3 * i + j] * groups[j], axis=1, keepdims=True) for j in range(3)] for i in range(3)]
+            around_me = [[None] * 3 for _ in range(3)]
+            around_me[1][1] = near[...]
+            for side in range(2):
+                around_me[2 * side][1] = yu_in[side, 3 * E:]
+                around_me[1][2 * side] = zu_in[side, 6 * E:]
+                for over in range(2):
+                    around_me[2 * side][2 * over] = du_in[2 * side + over, E:]
+            lifts = [[jnp.sum(around_me[i][j] * groups[j], axis=1, keepdims=True) for j in range(3)] for i in range(3)]
             maps = [[by_region([[x[f:f + 1] for x in row] for row in lifts], i) for i in range(3)] for f in range(3)]
             for t in range(TILES):
                 good = is_valid(label[t])
@@ -622,7 +632,7 @@
                 coarse_arrival(k, 0, d).wait_recv()
             group = group_sum(1)
             damping = damping_of(group)
-            lift = mask * jnp.sum(near[4] * group, axis=1, keepdims=True)
+            lift = mask * jnp.sum(near[...] * group, axis=1, keepdims=True)
             for f in range(3):
                 out[f] = out[f] + damping * (last_u[f] + lift[f:f + 1])
 
@@ -673,16 +683,16 @@
             V(inner, F32),
             V(inner[1:], F32),
             V((3, E, E * E), F32),
-            V((9, 8, 128), F32),
+            V((8, 128), F32),
             V((2, 3, E, 128), F32), V((2, 3, E, 128), F32),
-            V((2, 2 * E + 8, 128), F32), V((2, 2 * E + 8, 128), F32),
-            V((4, E + 8, 128), F32), V((4, E + 8, 128), F32),
-            V((2, 8 * E + 8, 128), F32), V((2, 8 * E + 8, 128), F32),
+            V((2, 2 * E, 128), F32), V((2, 2 * E, 128), F32),
+            V((4, E, 128), F32), V((4, E, 128), F32),
+            V((2, 8 * E, 128), F32), V((2, 8 * E, 128), F32),
             V((2, 6 * E, 128), F32), V((2, 6 * E, 128), F32),
             dma((14,)), dma((14,)),
-            V((2, 4 * E, 128), F32), V((2, 4 * E, 128), F32),
-            V((4, E, 128), F32), V((4, E, 128), F32),
-            V((2, 6 * E, 128), F32), V((2, 6 * E, 128), F32),
+            V((2, 3 * E + 8, 128), F32), V((2, 3 * E + 8, 128), F32),
+            V((4, E + 8, 128), F32), V((4, E + 8, 128), F32),
+            V((2, 6 * E + 8, 128), F32), V((2, 6 * E + 8, 128), F32),
             dma((8,)), dma((8,)),
             V((NEWTON, m, 8, 128), F32),
             dma((NEWTON, m)), dma((NEWTON, m)),

time: 34.5 us -> 33.6 us (0.974)
  Pallas kernels: 33.6 us -> 32.7 us
    pallas_call x1, Pallas kernels: 33.6 us -> 32.7 us  [shards(): pl.pallas_call(functools.partial(kernel, n, m), out_shape=V((3, E, E * E)...]
where the time goes in v4:
time: 33.6 us; the launch traced here: 33.4 us
  Pallas kernels  32.7 us (97%)
  local copies, waits for them, and re-layouts  0.75 us (2%)
    pallas_call x1, Pallas kernels, shards(): pl.pallas_call(functools.partial(kernel, n, m), out_shape=V((3, E, E * E)...  32.7 us
    unnamed x1, local copies, waits for them, and re-layouts  0.75 us

profile of v4, /device:TPU:0, one launch (start us, length us, event | category | flops | bytes accessed | tf_op | source)
XLA Modules:
  0.0 33.4 jit_solution(7757008804673676664)
XLA Ops:
  0.0 32.7 %shard_map.55 = f32[3,32,1024]{2,1,0:T(8,128)S(1)} custom-call(s32[1,3]{1,0:T(1,128)} %coords_in.1, f32[3,1,24]{2,1,0:T(1,128)} %bitcast.9, f32[3,32,1024]{2,1,0:T(8,128)} %bitcast.6, s32[32,1024]{1,0:T(8,128)} %bitcast.8, f32[3,32,1024]{2,1,0:T(8,128)} %bitcast.7), custom_call_target="tpu_custom_call" | custom-call | tf_op jit(solution)/shard_map/pallas_call | solution.py:665
  32.7 0.7 %copy.7 = f32[1,3,32,1024]{3,2,1,0:T(8,128)} copy(f32[1,3,32,1024]{3,2,1,0:T(8,128)S(1)} %bitcast.5) | data formatting | bytes 786432

commit v5 on v4

--- a/solution.py
+++ b/solution.py
@@ -208,6 +208,14 @@
             d_out[c] = corner_pack(tiles, over)
             du_out[c, E:] = mine
 
+    pl.semaphore_wait(barrier, greeted)
+    tell(0)
+    for c in range(4):
+        start(first_messages["d", c])
+    for name in ("misc", "state"):
+        for side in range(2):
+            start(first_messages[name, side])
+
     class View:
         def __init__(self, read, write):
             self.read, self.write = read, write
@@ -233,14 +241,6 @@
             for b in range(SMOOTH - 1):
                 upd[b, f, t, 0:PAD] = zero_rows
                 upd[b, f, t, PAD + E:] = zero_rows
-        for a, (view, raw) in enumerate(zip(views, raws)):
-            tile = jnp.full((E, 128), FAR if a == 3 else 0.0, F32)
-            for b in range(BLOCKS):
-                y = TILES * b + t - DEEP
-                if 0 <= y < E:
-                    moved = roll(raw(y // 4), WIDE * b + DEEP - 32 * (y % 4))
-                    tile = jnp.where(own_columns & (block == b), moved, tile)
-            view.write(t, tile)
 
     half_slots = WIDE // DEEP
 
@@ -295,12 +295,28 @@
                         moved = roll(got(side, a), first + DEEP - 32 * q)
                     view.write(t, jnp.where(here, moved, view.read(t)))
 
+    def widen(which):
+        for t in range(TILES):
+            for a in which:
+                tile = jnp.full((E, 128), FAR if a == 3 else 0.0, F32)
+                for b in range(BLOCKS):
+                    y = TILES * b + t - DEEP
+                    if 0 <= y < E:
+                        moved = roll(raws[a](y // 4), WIDE * b + DEEP - 32 * (y % 4))
+                        tile = jnp.where(own_columns & (block == b), moved, tile)
+                views[a].write(t, tile)
+
+    widen(range(4))
     for side in range(2):
         for i, tile in enumerate(z_pack(views[:4], side)):
             z_out[side, E * i:E * (i + 1)] = tile
-        zu_out[side, 6 * E:] = mine
+        start(first_messages["z", side])
+    widen(range(4, 7))
+    for side in range(2):
         for i, tile in enumerate(z_pack(views[4:], side)):
             zs_out[side, E * i:E * (i + 1)] = tile
+        start(first_messages["zs", side])
+        zu_out[side, 6 * E:] = mine
 
     far = jnp.full((E, 128), FAR, F32)
     none = jnp.zeros((8, 128), F32)
@@ -336,13 +352,6 @@
                 du_in[2 * side + over, 0:E] = blank
                 du_in[2 * side + over, E:] = none
 
-    pl.semaphore_wait(barrier, greeted)
-    tell(0)
-    for c in range(4):
-        start(first_messages["d", c])
-    for name in ("misc", "state", "z", "zs"):
-        for side in range(2):
-            start(first_messages[name, side])
 
     for side in range(2):
         arrive(first_messages["z", side])

time: 33.6 us -> 32.3 us (0.961)
  Pallas kernels: 32.7 us -> 31.4 us
    pallas_call x1, Pallas kernels: 32.7 us -> 31.4 us  [shards(): pl.pallas_call(functools.partial(kernel, n, m), out_shape=V((3, E, E * E)...]
where the time goes in v5:
time: 32.3 us; the launch traced here: 32.2 us
  Pallas kernels  31.4 us (97%)
  local copies, waits for them, and re-layouts  0.75 us (2%)
    pallas_call x1, Pallas kernels, shards(): pl.pallas_call(functools.partial(kernel, n, m), out_shape=V((3, E, E * E)...  31.4 us
    unnamed x1, local copies, waits for them, and re-layouts  0.75 us

profile of v5, /device:TPU:0, one launch (start us, length us, event | category | flops | bytes accessed | tf_op | source)
XLA Modules:
  0.0 32.2 jit_solution(14186170597629949117)
XLA Ops:
  0.0 31.4 %shard_map.55 = f32[3,32,1024]{2,1,0:T(8,128)S(1)} custom-call(s32[1,3]{1,0:T(1,128)} %coords_in.1, f32[3,1,24]{2,1,0:T(1,128)} %bitcast.9, f32[3,32,1024]{2,1,0:T(8,128)} %bitcast.6, s32[32,1024]{1,0:T(8,128)} %bitcast.8, f32[3,32,1024]{2,1,0:T(8,128)} %bitcast.7), custom_call_target="tpu_custom_call" | custom-call | tf_op jit(solution)/shard_map/pallas_call | solution.py:674
  31.4 0.7 %copy.7 = f32[1,3,32,1024]{3,2,1,0:T(8,128)} copy(f32[1,3,32,1024]{3,2,1,0:T(8,128)S(1)} %bitcast.5) | data formatting | bytes 786432

commit v6 on v5

--- a/solution.py
+++ b/solution.py
@@ -508,11 +508,8 @@
                 for f, (v, term) in enumerate(terms(u, tiles, t)):
                     later[f, t, PAD:PAD + E] = (1.0 - OMEGA) * v + term
 
-        def smooth(p, carry):
-            smooth_tiles(upd.at[jnp.where(p == 0, 0, 1 + lax.rem(p + 1, 2))], upd.at[1 + lax.rem(p, 2)], range(TILES))
-            return carry
-
-        lax.fori_loop(0, SMOOTH - 2, smooth, 0)
+        for p in range(SMOOTH - 2):
+            smooth_tiles(upd.at[0 if p == 0 else 1 + (p + 1) % 2], upd.at[1 + p % 2], range(TILES))
         u_last = upd.at[1 + (SMOOTH - 3) % 2]
         u = upd.at[1 + (SMOOTH - 2) % 2]
         u_views = [padded(u, f) for f in range(3)]

time: 32.3 us -> 31.8 us (0.985)
  Pallas kernels: 31.4 us -> 30.9 us
    pallas_call x1, Pallas kernels: 31.4 us -> 30.9 us  [shards(): pl.pallas_call(functools.partial(kernel, n, m), out_shape=V((3, E, E * E)...]
where the time goes in v6:
time: 31.8 us; the launch traced here: 31.7 us
  Pallas kernels  30.9 us (97%)
  local copies, waits for them, and re-layouts  0.75 us (2%)
    pallas_call x1, Pallas kernels, shards(): pl.pallas_call(functools.partial(kernel, n, m), out_shape=V((3, E, E * E)...  30.9 us
    unnamed x1, local copies, waits for them, and re-layouts  0.75 us

profile of v6, /device:TPU:0, one launch (start us, length us, event | category | flops | bytes accessed | tf_op | source)
XLA Modules:
  0.0 31.7 jit_solution(15734559000130007046)
XLA Ops:
  0.0 30.9 %shard_map.55 = f32[3,32,1024]{2,1,0:T(8,128)S(1)} custom-call(s32[1,3]{1,0:T(1,128)} %coords_in.1, f32[3,1,24]{2,1,0:T(1,128)} %bitcast.9, f32[3,32,1024]{2,1,0:T(8,128)} %bitcast.6, s32[32,1024]{1,0:T(8,128)} %bitcast.8, f32[3,32,1024]{2,1,0:T(8,128)} %bitcast.7), custom_call_target="tpu_custom_call" | custom-call | tf_op jit(solution)/shard_map/pallas_call | solution.py:671
  30.9 0.7 %copy.7 = f32[1,3,32,1024]{3,2,1,0:T(8,128)} copy(f32[1,3,32,1024]{3,2,1,0:T(8,128)S(1)} %bitcast.5) | data formatting | bytes 786432

commit v7 on v6

--- a/solution.py
+++ b/solution.py
@@ -470,7 +470,7 @@
                 square = square + jnp.where(mine_here, misfit * misfit, 0.0)
                 dg = 0.5 + 6.0 * conduct[f] + (0.25 * slope if f == 0 else slope)
                 w = weight / dg
-                if kind(t) != 1:
+                if k == 0 and kind(t) != 1:
                     scale[f, t] = w
                 upd[0, f, t, PAD:PAD + E] = -w * misfit
                 gain[f, t] = w * conduct[f]
@@ -644,7 +644,8 @@
 
         return carry
 
-    lax.fori_loop(0, NEWTON, sweep, 0)
+    for k in range(NEWTON):
+        sweep(k, 0)
 
     for spec in list(first_messages.values()) + list(update_messages.values()):
         left(spec)

time: 31.8 us -> 31.6 us (level)
  no operation moved by 1% of the time
where the time goes in v7:
time: 31.6 us; the launch traced here: 31.5 us
  Pallas kernels  30.7 us (97%)
  local copies, waits for them, and re-layouts  0.75 us (2%)
    pallas_call x1, Pallas kernels, shards(): pl.pallas_call(functools.partial(kernel, n, m), out_shape=V((3, E, E * E)...  30.7 us
    unnamed x1, local copies, waits for them, and re-layouts  0.75 us

profile of v7, /device:TPU:0, one launch (start us, length us, event | category | flops | bytes accessed | tf_op | source)
XLA Modules:
  0.0 31.5 jit_solution(12922430964950084145)
XLA Ops:
  0.0 30.7 %shard_map.55 = f32[3,32,1024]{2,1,0:T(8,128)S(1)} custom-call(s32[1,3]{1,0:T(1,128)} %coords_in.1, f32[3,1,24]{2,1,0:T(1,128)} %bitcast.9, f32[3,32,1024]{2,1,0:T(8,128)} %bitcast.6, s32[32,1024]{1,0:T(8,128)} %bitcast.8, f32[3,32,1024]{2,1,0:T(8,128)} %bitcast.7), custom_call_target="tpu_custom_call" | custom-call | tf_op jit(solution)/shard_map/pallas_call | solution.py:672
  30.7 0.7 %copy.7 = f32[1,3,32,1024]{3,2,1,0:T(8,128)} copy(f32[1,3,32,1024]{3,2,1,0:T(8,128)S(1)} %bitcast.5) | data formatting | bytes 786432
